TPU v7x, 512 devices: a whole 4x4x16 slice. The times are simulated.
512 devices in a mesh: seq: 64 (over z, x_lo, core), tp: 8 (over x_hi, y).
Axes of the slice: x: 4 (x_hi: 2, x_lo: 2; x = x_hi * 2 + x_lo), y: 4, z: 16, core: 2. Of those that a mesh axis runs over, the one named last changes fastest.
Arguments:
- query: bfloat16 [4096, 4096], P(('seq', 'tp')), may hold values from -150 to 150
- key_new: bfloat16 [4096, 1024], P(('seq', 'tp')), may hold values from -5 to 5
- value_new: bfloat16 [4096, 1024], P(('seq', 'tp')), may hold values from -6 to 6
- ssm_input: bfloat16 [4096, 8192], P(('seq', 'tp')), may hold values from -6 to 6
- ssm_gate: bfloat16 [4096, 8192], P(('seq', 'tp')), may hold values from -6 to 6
- ssm_b: bfloat16 [4096, 1024], P(('seq', 'tp')), may hold values from -4 to 4
- ssm_c: bfloat16 [4096, 1024], P(('seq', 'tp')), may hold values from -4 to 4
- log_decay: bfloat16 [4096, 128], P(('seq', 'tp')), may hold values from -0.8 to 0
- key_cache: bfloat16 [4096, 1024], P('seq', 'tp'), may hold values from -6 to 6
- value_cache: bfloat16 [4096, 1024], P('seq', 'tp'), may hold values from -6 to 6
- init_state: float32 [128, 64, 128], P('tp'), may hold values from -4 to 4
- skip_gain: float32 [128], P('tp'), may hold values from 0.3 to 1.5
- norm_gain: float32 [8192], P('tp'), may hold values from 0.5 to 1.5
- cache_length: int32 [1], replicated, may hold values from 1 to 4096
- span_start: int32 [1], replicated, may hold values from 0 to 255
Outputs:
- attn_output: bfloat16 [4096, 4096], P(('seq', 'tp'))
- ssm_output: bfloat16 [4096, 8192], P(('seq', 'tp'))
All inputs are finite; a program needn't handle non-finite values.
Results may differ from a plain program's by a relative error of at most 0.0095.
Values may be sent and summed in bfloat16 or wider, within the bound.
A program may use at most 128 MiB of HBM per device.

v0:
```python
import math

import jax
import jax.numpy as jnp
from jax import lax
from jax.sharding import PartitionSpec as P

HQ = 32
HK = 8
DH = 128
P_SIZE = 64
N = 128


def carried_in(shard, axis, combine, identity):
    count, position = (lax.axis_size(axis), lax.axis_index(axis))
    everything = jax.tree.map(
        lambda part, kind: lax.all_gather(part.astype(kind), axis),
        shard,
        (jnp.bfloat16, jnp.bfloat16),
    )
    start = jax.tree.map(
        lambda part, zero: jnp.broadcast_to(jnp.asarray(zero, part.dtype), part.shape),
        shard,
        identity,
    )

    def lap(k, before):
        reached = k < position
        new = combine(
            before, jax.tree.map(lambda part, own: part[k].astype(own.dtype), everything, shard)
        )
        return jax.tree.map(lambda a, b: jnp.where(reached, a, b), new, before)

    return lax.fori_loop(0, count, lap, start)


def attend(q_heads, k_heads, v_heads, key_cache, value_cache, cache_length, span_start):
    row_count = q_heads.shape[0]
    cache_rows = key_cache.shape[0]
    shard_rows = cache_rows + row_count
    kv_local = k_heads.shape[1] // DH
    ratio_heads = HQ // HK
    score_scale = 1.0 / math.sqrt(DH)
    query_places = lax.axis_index("seq") * row_count + jnp.arange(row_count, dtype=jnp.int32)
    queries = q_heads.reshape(row_count, kv_local, ratio_heads, DH)
    joined_keys = jnp.concatenate([key_cache, k_heads], 0)
    joined_values = jnp.concatenate([value_cache, v_heads], 0)

    def absorb(carried, key_block, value_block, row_start):
        block_len = key_block.shape[0]
        global_row = row_start + jnp.arange(block_len, dtype=jnp.int32)
        shard_number = global_row // shard_rows
        within = global_row % shard_rows
        from_cache = within < cache_rows
        cache_place = shard_number * cache_rows + within
        span_place = shard_number * row_count + within - cache_rows
        span_usable = (span_place[None, :] >= span_start[0]) & (
            span_place[None, :] <= query_places[:, None]
        )
        usable = jnp.where(
            from_cache[None, :], (cache_place < cache_length[0])[None, :], span_usable
        )

        def update(running):
            running_top, weight_sum, weighted = running
            scores = (
                jnp.einsum(
                    "jqxa,eqa->qxje",
                    queries,
                    key_block.reshape(block_len, kv_local, DH),
                    preferred_element_type=jnp.float32,
                )
                * score_scale
            )
            scores = jnp.where(usable[None, None], scores, -1e30)
            new_top = jnp.maximum(running_top, jnp.max(scores, axis=-1))
            weights = jnp.where(usable[None, None], jnp.exp(scores - new_top[..., None]), 0.0)
            shrink = jnp.exp(running_top - new_top)
            weight_sum = weight_sum * shrink + jnp.sum(weights, axis=-1)
            weighted = weighted * shrink[..., None] + jnp.einsum(
                "jefp,pja->jefa",
                weights.astype(jnp.bfloat16),
                value_block.reshape(block_len, kv_local, DH),
                preferred_element_type=jnp.float32,
            )
            return (new_top, weight_sum, weighted)

        def unchanged(running):
            return running

        return lax.cond(jnp.any(usable), update, unchanged, carried)

    start_top = jnp.full((kv_local, ratio_heads, row_count), -1e30, jnp.float32)
    start_sum = jnp.zeros((kv_local, ratio_heads, row_count), jnp.float32)
    start_weighted = jnp.zeros((kv_local, ratio_heads, row_count, DH), jnp.float32)
    carried = (start_top, start_sum, start_weighted)
    key_piece = lax.all_gather(joined_keys, "seq", axis=0, tiled=True)
    value_piece = lax.all_gather(joined_values, "seq", axis=0, tiled=True)
    piece_len = key_piece.shape[0]
    block_total = piece_len // shard_rows

    def step_block(running, block_args):
        key_block, value_block, block_number = block_args
        return (absorb(running, key_block, value_block, block_number * shard_rows), None)

    carried, unused = lax.scan(
        step_block,
        carried,
        (
            key_piece.reshape(block_total, shard_rows, key_piece.shape[1]),
            value_piece.reshape(block_total, shard_rows, value_piece.shape[1]),
            jnp.arange(block_total, dtype=jnp.int32),
        ),
    )
    final_top, weight_sum, weighted = carried
    mixed = weighted / weight_sum[..., None]
    return (
        jnp.transpose(mixed, (2, 0, 1, 3))
        .reshape(row_count, kv_local * ratio_heads * DH)
        .astype(jnp.bfloat16)
    )


def chain_states(earlier, later):
    earlier_log, earlier_state = earlier
    later_log, later_state = later
    return (
        earlier_log + later_log,
        jnp.exp(later_log)[:, None, None] * earlier_state + later_state,
    )


def mix_states(
    x_heads, z_heads, b_heads, c_heads, decay_heads, init_state, skip_gain, norm_gain, span_start
):
    highest = lax.Precision.HIGHEST
    row_count = x_heads.shape[0]
    head_count = decay_heads.shape[1]
    group_local = b_heads.shape[1] // N
    per_group = head_count // group_local
    sequence_locations = lax.axis_index("seq") * row_count + jnp.arange(row_count, dtype=jnp.int32)
    fading_exponent_amount = jnp.where(
        sequence_locations[:, None] >= span_start[0], decay_heads.astype(jnp.float32), 0.0
    )
    in_weight = jnp.sqrt(-jnp.expm1(2.0 * fading_exponent_amount))
    cum_decay = jnp.cumsum(fading_exponent_amount, axis=0)
    raw_inputs = x_heads.reshape(row_count, head_count, P_SIZE)
    weighted = raw_inputs.astype(jnp.float32) * in_weight[:, :, None]
    b_rows = b_heads.reshape(row_count, group_local, N)
    c_rows = c_heads.reshape(row_count, group_local, N)
    pair_score = jnp.einsum("tgn,sgn->gts", c_rows, b_rows, preferred_element_type=jnp.float32)
    pair_score = jnp.repeat(pair_score, per_group, axis=0)
    row_index = jnp.arange(row_count, dtype=jnp.int32)
    lower_mask = row_index[:, None] >= row_index[None, :]
    cum_heads = jnp.transpose(cum_decay)
    gaps = cum_heads[:, :, None] - cum_heads[:, None, :]
    gap_decay = jnp.where(lower_mask[None], jnp.exp(jnp.where(lower_mask[None], gaps, 0.0)), 0.0)
    intra = jnp.einsum("hts,shp->thp", pair_score * gap_decay, weighted, precision=highest)
    b_spread = jnp.repeat(b_rows.astype(jnp.float32), per_group, axis=1)
    c_spread = jnp.repeat(c_rows.astype(jnp.float32), per_group, axis=1)
    end_log = cum_decay[-1]
    to_end = jnp.exp(end_log[None, :] - cum_decay)
    local_state = jnp.einsum("sh,shp,shn->hpn", to_end, weighted, b_spread, precision=highest)
    empty_log = jnp.zeros((head_count,), jnp.float32)
    empty_state = jnp.zeros(local_state.shape, jnp.float32)
    prefix_log, prefix_state = carried_in(
        (end_log, local_state), "seq", chain_states, (empty_log, empty_state)
    )
    incoming = prefix_state + jnp.exp(prefix_log)[:, None, None] * init_state
    ssm_y = intra + jnp.exp(cum_decay)[:, :, None] * jnp.einsum(
        "thn,hpn->thp", c_spread, incoming, precision=highest
    )
    ssm_y = ssm_y + skip_gain[None, :, None] * raw_inputs.astype(jnp.float32)
    gated_y = ssm_y * jax.nn.silu(
        z_heads.reshape(row_count, head_count, P_SIZE).astype(jnp.float32)
    )
    grouped = gated_y.reshape(row_count, group_local, per_group * P_SIZE)
    mean_sq = jnp.mean(grouped * grouped, axis=-1, keepdims=True)
    normed = (
        grouped * lax.rsqrt(mean_sq + 1e-05) * norm_gain.reshape(group_local, per_group * P_SIZE)
    )
    return normed.reshape(row_count, head_count * P_SIZE).astype(jnp.bfloat16)


def local(
    query,
    key_new,
    value_new,
    ssm_input,
    ssm_gate,
    ssm_b,
    ssm_c,
    log_decay,
    key_cache,
    value_cache,
    init_state,
    skip_gain,
    norm_gain,
    cache_length,
    span_start,
):
    q_heads, k_heads, v_heads = (
        lax.all_to_all(query, "tp", split_axis=1, concat_axis=0, tiled=True),
        lax.all_to_all(key_new, "tp", split_axis=1, concat_axis=0, tiled=True),
        lax.all_to_all(value_new, "tp", split_axis=1, concat_axis=0, tiled=True),
    )
    attn_heads = attend(q_heads, k_heads, v_heads, key_cache, value_cache, cache_length, span_start)
    x_heads, z_heads, b_heads, c_heads, decay_heads = (
        lax.all_to_all(ssm_input, "tp", split_axis=1, concat_axis=0, tiled=True),
        lax.all_to_all(ssm_gate, "tp", split_axis=1, concat_axis=0, tiled=True),
        lax.all_to_all(ssm_b, "tp", split_axis=1, concat_axis=0, tiled=True),
        lax.all_to_all(ssm_c, "tp", split_axis=1, concat_axis=0, tiled=True),
        lax.all_to_all(log_decay, "tp", split_axis=1, concat_axis=0, tiled=True),
    )
    ssm_heads = mix_states(
        x_heads,
        z_heads,
        b_heads,
        c_heads,
        decay_heads,
        init_state,
        skip_gain,
        norm_gain,
        span_start,
    )
    attn_output, ssm_output = (
        lax.all_to_all(attn_heads, "tp", split_axis=0, concat_axis=1, tiled=True),
        lax.all_to_all(ssm_heads, "tp", split_axis=0, concat_axis=1, tiled=True),
    )
    return (attn_output, ssm_output)


def solution(mesh):
    placed = (
        P(("seq", "tp"), None),
        P(("seq", "tp"), None),
        P(("seq", "tp"), None),
        P(("seq", "tp"), None),
        P(("seq", "tp"), None),
        P(("seq", "tp"), None),
        P(("seq", "tp"), None),
        P(("seq", "tp"), None),
        P("seq", "tp"),
        P("seq", "tp"),
        P("tp", None, None),
        P("tp"),
        P("tp"),
        P(),
        P(),
    )
    return jax.shard_map(
        local,
        mesh=mesh,
        in_specs=placed,
        out_specs=(P(("seq", "tp"), None), P(("seq", "tp"), None)),
        check_vma=False,
    )
```

profile of v0, /device:TPU:483, one launch (start us, length us, event | category | flops | bytes accessed | tf_op | source)
XLA Modules:
  0.0 763.7 jit_solution(15803097157415811991)
XLA Ops:
  7.2 12.3 %all_to_all.157 = bf16[8,8,128]{2,0,1:T(8,128)(2,1)S(1)} all-to-all(bf16[8,8,128]{2,0,1:T(8,128)(2,1)} %bitcast.141), channel_id=1, replica_groups=mesh['seq'=64,'tp'=8] {'tp'}, dimensions={1} | all-to-all | bytes 32768 | tf_op jit(solution)/shard_map/all_to_all | solution.py:205
  20.9 9.8 %all_to_all.158 = bf16[8,8,128]{2,0,1:T(8,128)(2,1)S(1)} all-to-all(bf16[8,8,128]{2,0,1:T(8,128)(2,1)} %bitcast.142), channel_id=1, replica_groups=mesh['seq'=64,'tp'=8] {'tp'}, dimensions={1} | all-to-all | bytes 32768 | tf_op jit(solution)/shard_map/all_to_all | solution.py:206
  33.5 3.3 all-to-all-start.5
  37.5 5.8 all-to-all-done.5
  43.4 3.3 all-to-all-start.7
  47.0 6.2 all-to-all-done.7
  53.2 3.3 all-to-all-start.6
  56.7 63.5 %all-gather.1 = bf16[64,1,16]{2,1,0:T(2,128)(2,1)S(1)} all-gather(bf16[1,1,16]{2,1,0:T(2,128)(2,1)S(1)} %convert_bitcast_fusion.3), channel_id=1, replica_groups=mesh['seq'=64,'tp'=8] {'seq'}, dimensions={0}, use_global_device_ids=true | all-gather | bytes 2080 | tf_op jit(solution)/shard_map/all_gather | solution.py:18
  120.3 6.8 all-to-all-start.1
  127.2 6.6 all-to-all-done.1
  133.8 3.4 all-to-all-start.4
  137.2 6.8 all-to-all-done.4
  144.1 3.4 all-to-all-start.8
  147.9 6.4 all-to-all-done.8
  158.1 101.1 %all-gather.8.cloned.1.call-done = bf16[8192,128]{1,0:T(8,128)(2,1)} async-done(((bf16[128,128]{1,0:T(8,128)(2,1)}), bf16[8192,128]{1,0:T(8,128)(2,1)}) %all-gather.8.cloned.1.call-update) | async-done | bytes 2097168 | tf_op jit(solution)/shard_map/all_gather | solution.py:99
  259.3 401.0 %while.33 = (s32[]{:T(128)}, f32[1,4,64]{2,1,0:T(4,128)S(1)}, f32[1,4,64]{2,1,0:T(4,128)S(1)}, f32[1,4,64,128]{3,2,1,0:T(8,128)S(1)}, s32[64]{0:T(128)S(1)}, /*i...) while((s32[]{:T(128)}, f32[1,4,64]{2,1,0:T(4,128)S(1)}, ...), condition=%wide.region_6.7_spmd.clone, body=%wide.region_0.6_spmd.clone.sunk | while | flops 17179076 | bytes 839211 | solution.py:107
  269.5 2.3 conditional.3
  275.8 2.3 conditional.3
  294.6 2.3 conditional.3
  313.4 2.3 conditional.3
  319.7 2.3 conditional.3
  325.9 2.3 conditional.3
  338.5 2.3 conditional.3
  344.7 2.3 conditional.3
  363.5 2.3 conditional.3
  369.8 2.3 conditional.3
  382.4 2.3 conditional.3
  388.6 2.3 conditional.3
  413.7 2.3 conditional.3
  419.9 2.3 conditional.3
  426.2 2.3 conditional.3
  451.3 2.3 conditional.3
  457.5 2.3 conditional.3
  463.8 2.3 conditional.3
  488.9 2.3 conditional.3
  495.1 2.3 conditional.3
  501.4 2.3 conditional.3
  507.7 2.3 conditional.3
  532.7 2.3 conditional.3
  539.0 2.3 conditional.3
  545.2 2.3 conditional.3
  570.3 2.3 conditional.3
  576.6 2.3 conditional.3
  582.8 2.3 conditional.3
  661.1 5.6 all-to-all-start.3
  666.8 73.1 %while.34 = (s32[]{:T(128)}, f32[16]{0:T(128)S(1)}, f32[16,64,128]{2,1,0:T(8,128)S(1)}, s32[]{:T(128)}, bf16[64,16]{1,0:T(8,128)(2,1)S(1)}, /*index=5*/bf16[64,16,64,128]{3,2,1,0:T(8,128)(2,1)}, s32[]{:T(128)}, s32[]{:T(128)}) while((s32[]{:T(128)}, f32[16]{0:T(128)S(1)}, f32[16,64,128]{2,1,0:T(8,128)S(1)}, s32[]{:T(128)}, ...), condition=%wide.region_9.10_spmd.clone, body=%wide.region_8.9_spmd.clone.sunk | while | flops 655428 | bytes 1311123 | solution.py:35
  742.4 6.6 all-to-all-start.9
  749.0 6.9 all-to-all-done.9
  (998 shorter events, 478.9 us)
Async XLA Ops:
  7.2 150.9 %all-gather.6.cloned.1.call-start = ((), (), s32[]{:S(2)}) async-start(), calls=%async_computation.10 | async-start | bytes 2129920 | tf_op jit(solution)/shard_map/all_gather | solution.py:98
  20.9 238.3 %all-gather.8.cloned.1.call-start = ((), (), s32[]{:S(2)}) async-start(), calls=%async_computation.11 | async-start | bytes 2129920 | tf_op jit(solution)/shard_map/all_gather | solution.py:99
  33.5 9.9 %all-to-all-start.5 = ((bf16[8,8,16]{2,0,1:T(8,128)(2,1)}), bf16[8,8,16]{2,0,1:T(8,128)(2,1)S(1)}, u32[]{:S(2)}, u32[]{:S(2)}) async-start(bf16[8,8,16]{2,0,1:T(8,128)(2,1)} %copy.86), calls=%async_computation.5 | async-start | bytes 32768 | tf_op jit(solution)/shard_map/all_to_all | solution.py:214
  43.4 9.8 %all-to-all-start.7 = ((bf16[8,8,128]{2,0,1:T(8,128)(2,1)}), bf16[8,8,128]{2,0,1:T(8,128)(2,1)S(1)}, u32[]{:S(2)}, u32[]{:S(2)}) async-start(bf16[8,8,128]{2,0,1:T(8,128)(2,1)} %bitcast.143), calls=%async_computation.7 | async-start | bytes 32768 | tf_op jit(solution)/shard_map/all_to_all | solution.py:212
  53.2 67.1 %all-to-all-start.6 = ((bf16[8,8,128]{2,0,1:T(8,128)(2,1)}), bf16[8,8,128]{2,0,1:T(8,128)(2,1)S(1)}, u32[]{:S(2)}, u32[]{:S(2)}) async-start(bf16[8,8,128]{2,0,1:T(8,128)(2,1)} %bitcast.144), calls=%async_computation.6 | async-start | bytes 32768 | tf_op jit(solution)/shard_map/all_to_all | solution.py:213
  120.3 13.5 %all-to-all-start.1 = ((bf16[8,8,512]{2,0,1:T(8,128)(2,1)}), bf16[8,8,512]{2,0,1:T(8,128)(2,1)S(1)}, u32[]{:S(2)}, u32[]{:S(2)}) async-start(bf16[8,8,512]{2,0,1:T(8,128)(2,1)} %bitcast.137), calls=%async_computation.1 | async-start | bytes 131072 | tf_op jit(solution)/shard_map/all_to_all | solution.py:204
  133.8 10.3 %all-to-all-start.4 = ((bf16[8,8,1024]{2,0,1:T(8,128)(2,1)}), bf16[8,8,1024]{2,0,1:T(8,128)(2,1)S(1)}, u32[]{:S(2)}, u32[]{:S(2)}) async-start(bf16[8,8,1024]{2,0,1:T(8,128)(2,1)} %bitcast.133), calls=%async_computation.4 | async-start | bytes 262144 | tf_op jit(solution)/shard_map/all_to_all | solution.py:210
  144.1 10.3 %all-to-all-start.8 = ((bf16[8,8,1024]{2,0,1:T(8,128)(2,1)}), bf16[8,8,1024]{2,0,1:T(8,128)(2,1)S(1)}, u32[]{:S(2)}, u32[]{:S(2)}) async-start(bf16[8,8,1024]{2,0,1:T(8,128)(2,1)} %bitcast.134), calls=%async_computation.8 | async-start | bytes 262144 | tf_op jit(solution)/shard_map/all_to_all | solution.py:211
  147.4 519.3 %all-gather.10.cloned.1.call-start = ((), (), s32[]{:S(2)}) async-start(), calls=%async_computation.12 | async-start | bytes 17039360 | tf_op jit(solution)/shard_map/all_gather | solution.py:18
  661.1 81.2 %all-to-all-start.3 = ((bf16[8,8,512]{2,1,0:T(8,128)(2,1)}), bf16[8,8,512]{2,1,0:T(8,128)(2,1)S(1)}, u32[]{:S(2)}, u32[]{:S(2)}) async-start(bf16[8,8,512]{2,1,0:T(8,128)(2,1)} %convert_element_type.104), calls=%async_computation.3 | async-start | bytes 131072 | tf_op jit(solution)/shard_map/all_to_all | solution.py:228
  666.8 73.2 %copy-start.1 = (f32[16,64,128]{2,1,0:T(8,128)S(1)}, f32[16,64,128]{2,1,0:T(8,128)}, u32[]{:S(2)}) copy-start(f32[16,64,128]{2,1,0:T(8,128)} %param.31) | copy-start | bytes 1572868
  666.8 73.1 %copy-start.2 = (f32[16]{0:T(128)S(1)}, f32[16]{0:T(128)}, u32[]{:S(2)}) copy-start(f32[16]{0:T(128)} %param.32) | copy-start | bytes 196
  739.9 1.7 copy-start
  742.4 13.6 %all-to-all-start.9 = ((bf16[8,8,1024]{2,1,0:T(8,128)(2,1)}), bf16[8,8,1024]{2,1,0:T(8,128)(2,1)S(1)}, u32[]{:S(2)}, u32[]{:S(2)}) async-start(bf16[8,8,1024]{2,1,0:T(8,128)(2,1)} %multiply_convert_fusion), calls=%async_computation.9 | async-start | bytes 262144 | tf_op jit(solution)/shard_map/all_to_all | solution.py:229
Sparse Core Ops, SparseCore 0:
  21.0 116.9 all-gather.5
  140.8 118.4 all-gather.7
  261.4 135.8 all-gather.9
where the time goes:
time: 778 us; the launch traced here: 764 us
  other arithmetic  220 us (28%)
  waiting for transfers between devices  140 us (18%)
  matrix products  134 us (17%)
  loops' own time  90.7 us (12%)
  blocking collectives  85.6 us (11%)
  local copies, waits for them, and re-layouts  42.9 us (6%)
  starting transfers between devices  35.9 us (5%)
  between operations  14.7 us (2%)
    all_gather x1, waiting for transfers between devices, attend(): value_piece = lax.all_gather(joined_values, 'seq', axis=0, tiled=True)  101 us
    another operation x1, loops' own time, attend(): lax.scan(step_block, carried, (key_piece.reshape(block_total, shard_rows,...  86.3 us
    ge x64, other arithmetic, absorb(): span_place[None, :] >= span_start[0]  83.9 us
    select_n x64, other arithmetic, lap(): return jax.tree.map(lambda a, b: jnp.where(reached, a, b), new, before)  70.1 us
    dot_general x64, matrix products, update(): jnp.einsum('jqxa,eqa->qxje', queries, key_block.reshape(block_len, kv_loc...  66.2 us
    all_gather x1, blocking collectives, carried_in(): lax.all_gather(part.astype(kind), axis)  63.5 us
    dot_general x64, matrix products, update(): jnp.einsum('jefp,pja->jefa', weights.astype(jnp.bfloat16), value_block.re...  63.2 us
    reduce_or x64, other arithmetic, absorb(): return lax.cond(jnp.any(usable), update, unchanged, carried)  45.6 us
  transfers between devices with their start and end apart: 11, of which 7 were waited for; matrix products, arithmetic and copies ran while one was open for 52% of the time, Pallas kernels for 0%

commit v1 on v0

v1 whole, which is shorter than its diff:
```python
import jax
import jax.numpy as jnp
from jax import lax
from jax.experimental import pallas as pl
from jax.experimental.pallas import tpu as pltpu
from jax.sharding import PartitionSpec as P

Z = 16
LANES = 4
TP = 8
PLANE = LANES * TP
DH = 128
P_SIZE = 64
SPAN = 256
KEYS = 1024
ROWS = 1024
UNIT = 256
UP = 8
DOWN = 7
SCALE = 128.0 ** -0.5
LOW = -1e30
MESH = pl.DeviceIdType.MESH
F32 = jnp.float32
BF16 = jnp.bfloat16


def dot(a, b, ca, cb):
    return lax.dot_general(a, b, (((ca,), (cb,)), ((), ())), preferred_element_type=F32)


def kernel(
    length_ref, start_ref, q_ref, k_ref, v_ref, xw_ref, dec_ref, b_ref, c_ref,
    kc_ref, vc_ref, init_ref, gain_ref, x_ref, gate_ref,
    attn_ref, ssm_ref,
    a_send, a_recv, kv_send, kv_recv, g_recv, cache, fresh, states,
    cum_ref, y_ref, prior, o1, m1, l1, e_send, e_recv, s_send, s_recv,
    a_ss, a_rs, kv_ss, kv_rs, g_ss, g_rs,
    up_ss, up_rs, dn_ss, dn_rs, e_ss, e_rs, s_ss, s_rs,
):
    seq, tp = lax.axis_index("seq"), lax.axis_index("tp")
    z, lane = seq // LANES, lax.rem(seq, LANES)
    me = lane * TP + tp
    above = lax.rem(z + 1, Z) * LANES + lane
    below = lax.rem(z + Z - 1, Z) * LANES + lane

    def place(d):
        return (z * LANES + d // TP, lax.rem(d, TP))

    barrier = pltpu.get_barrier_semaphore()

    def greet(i, unused):
        pl.semaphore_signal(
            barrier, inc=1, device_id=place(lax.rem(me + i, PLANE)), device_id_type=MESH
        )
        return unused

    lax.fori_loop(1, PLANE, greet, 0)
    for other in (above, below):
        pl.semaphore_signal(barrier, inc=1, device_id=(other, tp), device_id_type=MESH)

    cache[z, 0:64, :] = kc_ref[...]
    cache[z, 64:128, :] = vc_ref[...]
    q = q_ref[...].astype(F32)
    xw = xw_ref[...].astype(F32)
    dec = dec_ref[...].astype(F32)
    bb = b_ref[...].astype(F32)
    cc = c_ref[...].astype(F32)
    kk = k_ref[...].astype(F32)
    vv = v_ref[...].astype(F32)

    def columns(a, first, count):
        return jnp.concatenate(
            [a[:, (first + j) * 128:(first + j + 1) * 128] for j in range(count)], 0
        ).astype(BF16)

    for t in range(TP):
        q_block = columns(q, t * 4, 4)
        bc_block = jnp.concatenate(
            [bb[:, t * 128:(t + 1) * 128], cc[:, t * 128:(t + 1) * 128]], 0
        ).astype(BF16)
        kv_send[t] = jnp.concatenate(
            [kk[:, t * 128:(t + 1) * 128], vv[:, t * 128:(t + 1) * 128]], 0
        ).astype(BF16)
        for l in range(LANES):
            d = l * TP + t
            a_send[d, 0:32, :] = q_block
            a_send[d, 32:48, :] = columns(xw, t * 8 + l * 2, 2)
            a_send[d, 48:64, :] = columns(dec, t * 8 + l * 2, 2)
            a_send[d, 64:80, :] = bc_block
    a_recv[me] = a_send[me]
    kv_recv[tp] = kv_send[tp]
    g_recv[tp] = gain_ref[...]
    pl.semaphore_wait(barrier, PLANE - 1 + 2)

    def up_copy(buf, ring, step):
        block = lax.rem(z + Z - step, Z)
        return pltpu.make_async_remote_copy(
            src_ref=buf.at[block], dst_ref=buf.at[block],
            send_sem=up_ss.at[ring, step], recv_sem=up_rs.at[ring, step],
            device_id=(above, tp), device_id_type=MESH,
        )

    def dn_copy(buf, ring, step):
        block = lax.rem(z + step, Z)
        return pltpu.make_async_remote_copy(
            src_ref=buf.at[block], dst_ref=buf.at[block],
            send_sem=dn_ss.at[ring, step], recv_sem=dn_rs.at[ring, step],
            device_id=(below, tp), device_id_type=MESH,
        )

    def up_wait(buf, ring, step):
        block = lax.rem(z + 2 * Z - 1 - step, Z)
        pltpu.make_async_remote_copy(
            src_ref=buf.at[block], dst_ref=buf.at[block],
            send_sem=up_ss.at[ring, step], recv_sem=up_rs.at[ring, step],
            device_id=(above, tp), device_id_type=MESH,
        ).wait_recv()

    def dn_wait(buf, ring, step):
        block = lax.rem(z + 1 + step, Z)
        pltpu.make_async_remote_copy(
            src_ref=buf.at[block], dst_ref=buf.at[block],
            send_sem=dn_ss.at[ring, step], recv_sem=dn_rs.at[ring, step],
            device_id=(below, tp), device_id_type=MESH,
        ).wait_recv()

    def first(buf, ring):
        up_copy(buf, ring, 0).start()
        dn_copy(buf, ring, 0).start()

    def tick(buf, ring, step):
        up_wait(buf, ring, step - 1)
        if step < UP:
            up_copy(buf, ring, step).start()
        if step <= DOWN:
            dn_wait(buf, ring, step - 1)
        if step < DOWN:
            dn_copy(buf, ring, step).start()

    def sent(buf, ring):
        for step in range(UP):
            up_copy(buf, ring, step).wait_send()
        for step in range(DOWN):
            dn_copy(buf, ring, step).wait_send()

    def kv_copy(t, slot):
        return pltpu.make_async_remote_copy(
            src_ref=kv_send.at[t], dst_ref=kv_recv.at[slot],
            send_sem=kv_ss.at[t], recv_sem=kv_rs.at[slot],
            device_id=(seq, t), device_id_type=MESH,
        )

    def g_copy(t, slot):
        return pltpu.make_async_remote_copy(
            src_ref=gain_ref, dst_ref=g_recv.at[slot],
            send_sem=g_ss.at[t], recv_sem=g_rs.at[slot],
            device_id=(seq, t), device_id_type=MESH,
        )

    def a_copy(d, slot):
        return pltpu.make_async_remote_copy(
            src_ref=a_send.at[d], dst_ref=a_recv.at[slot],
            send_sem=a_ss.at[d], recv_sem=a_rs.at[slot],
            device_id=place(d), device_id_type=MESH,
        )

    def e_copy(d, slot):
        return pltpu.make_async_remote_copy(
            src_ref=e_send.at[d], dst_ref=e_recv.at[slot],
            send_sem=e_ss.at[d], recv_sem=e_rs.at[slot],
            device_id=place(d), device_id_type=MESH,
        )

    def s_copy(d, slot):
        return pltpu.make_async_remote_copy(
            src_ref=s_send.at[d], dst_ref=s_recv.at[slot],
            send_sem=s_ss.at[d], recv_sem=s_rs.at[slot],
            device_id=place(d), device_id_type=MESH,
        )

    def over_plane(act):
        def body(i, unused):
            act(lax.rem(me + i, PLANE))
            return unused

        lax.fori_loop(1, PLANE, body, 0)

    def over_tp(act):
        def body(i, unused):
            act(lax.rem(tp + i, TP))
            return unused

        lax.fori_loop(1, TP, body, 0)

    first(cache, 0)
    over_tp(lambda t: kv_copy(t, tp).start())
    over_plane(lambda d: a_copy(d, me).start())
    over_tp(lambda t: g_copy(t, tp).start())

    prior[...] = jnp.transpose(
        init_ref[pl.ds(lane * 4, 4)].reshape(4 * P_SIZE, 128)
    )
    for step in range(1, 4):
        tick(cache, 0, step)

    over_tp(lambda t: kv_copy(t, t).wait_recv())
    kv = kv_recv[...].astype(F32)
    fresh[z, 0:64, :] = kv[:, 0:8, :].reshape(64, DH).astype(BF16)
    fresh[z, 64:128, :] = kv[:, 8:16, :].reshape(64, DH).astype(BF16)
    first(fresh, 1)
    tick(cache, 0, 4)
    over_plane(lambda d: a_copy(d, d).wait_recv())

    def halves(first_row):
        part = a_recv[:, first_row:first_row + 16, :].astype(F32)
        return part[:, 0:8, :].reshape(SPAN, 128), part[:, 8:16, :].reshape(SPAN, 128)

    b_all, c_all = halves(64)
    b_all, c_all = b_all.astype(BF16), c_all.astype(BF16)
    x_all = jnp.concatenate(halves(32), 1)
    d_all = jnp.concatenate(halves(48), 1).astype(BF16)
    row = lax.broadcasted_iota(jnp.int32, (SPAN, SPAN), 0)
    col = lax.broadcasted_iota(jnp.int32, (SPAN, SPAN), 1)
    lower = row >= col
    ones = lower.astype(F32).astype(BF16)
    cum = dot(ones, d_all, 1, 0)
    end = cum[SPAN - 1:SPAN, :]
    local = dot(b_all, (x_all * jnp.exp(end - cum)).astype(BF16), 0, 0)
    states[z, 0:128, :] = local.astype(BF16)
    high = end.astype(BF16).astype(F32)
    states[z, 128:144, :] = jnp.concatenate(
        [jnp.broadcast_to(high, (8, SPAN)), jnp.broadcast_to(end - high, (8, SPAN))], 0
    ).astype(BF16)
    first(states, 2)
    cum_ref[...] = cum

    x_all = x_all.astype(BF16)
    cum_t = dot(d_all, ones, 0, 1)
    pair = dot(c_all, b_all, 1, 1)
    first_half = lax.broadcasted_iota(jnp.int32, (SPAN, 128), 1) < P_SIZE
    for half in range(2):
        parts = []
        for j in (2 * half, 2 * half + 1):
            gap = cum[:, j * P_SIZE:j * P_SIZE + 1] - cum_t[j * P_SIZE:j * P_SIZE + 1, :]
            fade = jnp.where(lower, jnp.exp(jnp.where(lower, gap, 0.0)), 0.0)
            parts.append(
                dot((pair * fade).astype(BF16), x_all[:, half * 128:(half + 1) * 128], 1, 0)
            )
            tick(cache, 0, 5 + j)
            tick(fresh, 1, 1 + j)
            tick(states, 2, 1 + j)
        y_ref[:, half * 128:(half + 1) * 128] = jnp.where(first_half, parts[0], parts[1])

    key_at = lax.broadcasted_iota(jnp.int32, (1, KEYS), 1)
    key_place = (key_at // 64) * SPAN + lane * 64 + lax.rem(key_at, 64)
    row_at = lax.broadcasted_iota(jnp.int32, (UNIT, 1), 0)

    def part(u, buf, usable):
        queries = a_recv[pl.ds(u * 8, 8), 0:32, :].reshape(UNIT, DH)
        keys = buf[:, 0:64, :].reshape(KEYS, DH)
        values = buf[:, 64:128, :].reshape(KEYS, DH)
        scores = jnp.where(usable, dot(queries, keys, 1, 1) * SCALE, LOW)
        top = jnp.max(scores, axis=1, keepdims=True)
        weights = jnp.exp(scores - top)
        total = jnp.sum(weights, axis=1, keepdims=True)
        return top, total, dot(weights.astype(BF16), values, 1, 0)

    cached = key_place < length_ref[0]
    for u in range(ROWS // UNIT):
        top, total, mixed = part(u, cache, cached)
        m1[u * UNIT:(u + 1) * UNIT, :] = top
        l1[u * UNIT:(u + 1) * UNIT, :] = total
        o1[u * UNIT:(u + 1) * UNIT, :] = mixed
        tick(fresh, 1, 5 + u)
        tick(states, 2, 5 + u)

    def lap(k, unused):
        tail = states[k, 128:144, :].astype(F32)
        log = tail[0:1, :] + tail[8:9, :]
        prior[...] = prior[...] * jnp.exp(log) + states[k, 0:128, :].astype(F32)
        return unused

    lax.fori_loop(0, z, lap, 0)
    y = y_ref[...] + jnp.exp(cum_ref[...]) * dot(c_all, prior[...].astype(BF16), 1, 0)
    e_send[:, 32:48, :] = jnp.concatenate(
        [y[:, 0:128].reshape(PLANE, 8, 128), y[:, 128:256].reshape(PLANE, 8, 128)], 1
    ).astype(BF16)

    spot = (
        lax.broadcasted_iota(jnp.int32, (1, 32, 128), 1)
        == lax.broadcasted_iota(jnp.int32, (1, 32, 128), 2)
    ).astype(F32)
    for u in range(ROWS // UNIT):
        query_place = z * SPAN + u * 64 + (row_at // 32) * 8 + lax.rem(row_at, 8)
        usable = (key_place >= start_ref[0]) & (key_place <= query_place)
        top, total, mixed = part(u, fresh, usable)
        top1, total1 = m1[u * UNIT:(u + 1) * UNIT, :], l1[u * UNIT:(u + 1) * UNIT, :]
        both = jnp.maximum(top, top1)
        by, by1 = jnp.exp(top - both), jnp.exp(top1 - both)
        total = total * by + total1 * by1
        mixed = (mixed * by + o1[u * UNIT:(u + 1) * UNIT, :] * by1) / total
        e_send[u * 8:(u + 1) * 8, 0:32, :] = mixed.astype(BF16).reshape(8, 32, DH)
        size = jnp.broadcast_to(both + jnp.log(total), (UNIT, 128)).reshape(8, 32, 128)
        s_send[u * 8:(u + 1) * 8] = jnp.broadcast_to(
            jnp.sum(size * spot, axis=1, keepdims=True), (8, 8, 128)
        )

    e_recv[me] = e_send[me]
    s_recv[me] = s_send[me]
    over_plane(lambda d: s_copy(d, me).start())
    over_plane(lambda d: e_copy(d, me).start())
    over_tp(lambda t: g_copy(t, t).wait_recv())
    over_plane(lambda d: s_copy(d, d).wait_recv())
    over_plane(lambda d: e_copy(d, d).wait_recv())

    for t in range(TP):
        sizes = [
            jnp.sum(s_recv[l * TP + t, 0:1, :] * spot[0], axis=1, keepdims=True)
            for l in range(LANES)
        ]
        most = jnp.maximum(jnp.maximum(sizes[0], sizes[1]), jnp.maximum(sizes[2], sizes[3]))
        shares = [jnp.exp(size - most) for size in sizes]
        whole = shares[0] + shares[1] + shares[2] + shares[3]
        out = sum(
            share * e_recv[l * TP + t, 0:32, :].astype(F32) for l, share in enumerate(shares)
        ) / whole
        for h in range(4):
            at = (t * 4 + h) * 128
            attn_ref[:, at:at + 128] = out[h * 8:(h + 1) * 8, :].astype(BF16)

        gated, squares = [], 0.0
        for l in range(LANES):
            y_part = e_recv[l * TP + t, 32:48, :].astype(F32)
            for half in range(2):
                r = l * 2 + half
                at = t * 1024 + r * 128
                gate = gate_ref[:, at:at + 128].astype(F32)
                value = y_part[half * 8:(half + 1) * 8, :] + g_recv[
                    t, 8 + r:9 + r, :
                ] * x_ref[:, at:at + 128].astype(F32)
                value = value * (gate / (1.0 + jnp.exp(-gate)))
                squares = squares + value * value
                gated.append(value)
        scale = lax.rsqrt(jnp.sum(squares, axis=1, keepdims=True) * (1.0 / 1024) + 1e-5)
        for r in range(8):
            at = t * 1024 + r * 128
            ssm_ref[:, at:at + 128] = (gated[r] * scale * g_recv[t, r:r + 1, :]).astype(BF16)

    over_tp(lambda t: kv_copy(t, tp).wait_send())
    over_tp(lambda t: g_copy(t, tp).wait_send())
    over_plane(lambda d: a_copy(d, me).wait_send())
    over_plane(lambda d: s_copy(d, me).wait_send())
    over_plane(lambda d: e_copy(d, me).wait_send())
    sent(cache, 0)
    sent(fresh, 1)
    sent(states, 2)


def local(
    query, key_new, value_new, ssm_input, ssm_gate, ssm_b, ssm_c, log_decay,
    key_cache, value_cache, init_state, skip_gain, norm_gain, cache_length, span_start,
):
    token = (lax.axis_index("seq") * TP + lax.axis_index("tp")) * 8 + jnp.arange(8)
    decay = jnp.where(token[:, None] >= span_start[0], log_decay.astype(F32), 0.0)
    in_weight = jnp.sqrt(-jnp.expm1(2.0 * decay))
    weighted = (
        (ssm_input.reshape(8, 128, P_SIZE).astype(F32) * in_weight[:, :, None])
        .reshape(8, 8192)
        .astype(BF16)
    )
    spread = jnp.repeat(decay.astype(BF16), P_SIZE, axis=1)
    gains = jnp.concatenate(
        [norm_gain.reshape(8, 128), jnp.repeat(skip_gain, P_SIZE).reshape(8, 128)], 0
    )
    vmem = pl.BlockSpec(memory_space=pltpu.VMEM)
    smem = pl.BlockSpec(memory_space=pltpu.SMEM)
    dma = pltpu.SemaphoreType.DMA
    return pl.pallas_call(
        kernel,
        out_shape=(
            jax.ShapeDtypeStruct((8, 4096), BF16),
            jax.ShapeDtypeStruct((8, 8192), BF16),
        ),
        in_specs=[smem] * 2 + [vmem] * 13,
        out_specs=(vmem, vmem),
        scratch_shapes=[
            pltpu.VMEM((PLANE, 80, 128), BF16),
            pltpu.VMEM((PLANE, 80, 128), BF16),
            pltpu.VMEM((TP, 16, 128), BF16),
            pltpu.VMEM((TP, 16, 128), BF16),
            pltpu.VMEM((TP, 16, 128), F32),
            pltpu.VMEM((Z, 128, DH), BF16),
            pltpu.VMEM((Z, 128, DH), BF16),
            pltpu.VMEM((Z, 144, SPAN), BF16),
            pltpu.VMEM((SPAN, SPAN), F32),
            pltpu.VMEM((SPAN, SPAN), F32),
            pltpu.VMEM((128, SPAN), F32),
            pltpu.VMEM((ROWS, DH), F32),
            pltpu.VMEM((ROWS, 1), F32),
            pltpu.VMEM((ROWS, 1), F32),
            pltpu.VMEM((PLANE, 48, 128), BF16),
            pltpu.VMEM((PLANE, 48, 128), BF16),
            pltpu.VMEM((PLANE, 8, 128), F32),
            pltpu.VMEM((PLANE, 8, 128), F32),
            dma((PLANE,)), dma((PLANE,)),
            dma((TP,)), dma((TP,)),
            dma((TP,)), dma((TP,)),
            dma((3, UP)), dma((3, UP)),
            dma((3, DOWN)), dma((3, DOWN)),
            dma((PLANE,)), dma((PLANE,)),
            dma((PLANE,)), dma((PLANE,)),
        ],
        compiler_params=pltpu.CompilerParams(
            collective_id=0, has_side_effects=True, vmem_limit_bytes=40 * 1024 * 1024
        ),
        name="mixers",
    )(
        cache_length, span_start, query, key_new, value_new, weighted, spread, ssm_b, ssm_c,
        key_cache, value_cache, init_state, gains, ssm_input, ssm_gate,
    )


def solution(mesh):
    rows = P(("seq", "tp"), None)
    placed = (rows,) * 8 + (
        P("seq", "tp"),
        P("seq", "tp"),
        P("tp", None, None),
        P("tp"),
        P("tp"),
        P(),
        P(),
    )
    return jax.shard_map(
        local, mesh=mesh, in_specs=placed, out_specs=(rows, rows), check_vma=False
    )
```

time: 778 us -> 80.6 us (0.10)
  the two profiles are of different devices: /device:TPU:483 before, /device:TPU:1 now
where the time goes in v1:
time: 80.6 us; the launch traced here: 80.3 us
  Pallas kernels  74 us (92%)
  local copies, waits for them, and re-layouts  4.11 us (5%)
  between operations  2.12 us (3%)
    pallas_call x1, Pallas kernels, local(): pl.pallas_call(kernel, out_shape=(jax.ShapeDtypeStruct((8, 4096), BF16),...  74 us
    unnamed x28, local copies, waits for them, and re-layouts  3.02 us

profile of v1, /device:TPU:1, one launch (start us, length us, event | category | flops | bytes accessed | tf_op | source)
XLA Modules:
  0.0 80.3 jit_solution(14313666864345099262)
XLA Ops:
  1.3 0.0 copy-start.11
  1.3 0.7 copy-done.11
  2.0 0.1 fusion
  2.0 0.2 mul.27
  2.3 0.0 copy-start.1
  2.3 0.2 mul.28
  2.5 0.7 copy-done.1
  3.2 0.0 copy-start
  3.2 0.2 broadcast_in_dim.26
  3.4 0.0 copy-start.12
  3.4 0.0 copy-start.10
  3.4 0.0 copy-start.2
  3.4 0.0 copy-start.3
  3.5 0.0 copy-start.7
  3.5 0.0 copy-start.8
  3.5 0.0 copy-start.9
  3.5 0.3 reshape.22.dec_ref
  3.8 0.3 copy-done.12
  4.1 0.0 copy-start.6
  4.1 0.1 broadcast_in_dim.27
  4.1 0.0 copy-start.5
  4.1 0.1 broadcast_in_dim.28
  4.2 0.0 copy-start.4
  4.2 0.1 broadcast_in_dim.29
  4.3 0.0 copy-done.10
  5.0 0.0 copy-done
  5.0 0.0 copy-done.2
  5.0 0.0 copy-done.3
  5.0 0.0 copy-done.7
  5.0 0.0 copy-done.8
  5.0 0.0 copy-done.9
  5.0 0.0 copy-done.6
  5.0 0.0 copy-done.5
  5.0 0.0 copy-done.4
  5.1 74.0 %mixers.1 = (bf16[8,4096]{1,0:T(8,128)(2,1)S(1)}, bf16[8,8192]{1,0:T(8,128)(2,1)S(1)}) custom-call(s32[1]{0:T(128)S(6)} %copy.19.length_ref, s32[1]{0:T(128)} %copy.20.start_ref, bf16[8,4096]{1,0:T(8,128)(2,1)S(1)} %copy-done.3, bf16[8,1024]{1,0:T(8,128)(2,1)S(1)} %copy-done.4, bf16[8,1024]{1,0:T(8,128)(2,1)S(1)} %copy-done.5, ...), custom_call_target="tpu_custom_call" | custom-call | tf_op jit(solution)/shard_map/mixers/pallas_call | solution.py:378
  79.0 0.6 copy.21
  79.7 0.7 copy.22
  (3 shorter events, 0.0 us)
Async XLA Ops:
  1.3 0.7 copy-start.11
  2.3 0.9 %copy-start.1 = (bf16[8,8192]{1,0:T(8,128)(2,1)S(1)}, bf16[8,8192]{1,0:T(8,128)(2,1)}, u32[]{:S(2)}) copy-start(bf16[8,8192]{1,0:T(8,128)(2,1)} %x_ref.1) | copy-start | bytes 393220
  3.2 1.8 %copy-start = (f32[16,64,128]{2,1,0:T(8,128)S(1)}, f32[16,64,128]{2,1,0:T(8,128)}, u32[]{:S(2)}) copy-start(f32[16,64,128]{2,1,0:T(8,128)} %init_ref.1) | copy-start | bytes 1572868
  3.4 0.7 copy-start.12
  3.4 0.9 %copy-start.10 = (f32[1024]{0:T(1024)S(1)}, f32[1024]{0:T(1024)}, u32[]{:S(2)}) copy-start(f32[1024]{0:T(1024)} %param.27) | copy-start | bytes 12292
  3.4 1.5 %copy-start.2 = (bf16[8,8192]{1,0:T(8,128)(2,1)S(1)}, bf16[8,8192]{1,0:T(8,128)(2,1)}, u32[]{:S(2)}) copy-start(bf16[8,8192]{1,0:T(8,128)(2,1)} %gate_ref.1) | copy-start | bytes 393220
  3.4 1.5 %copy-start.3 = (bf16[8,4096]{1,0:T(8,128)(2,1)S(1)}, bf16[8,4096]{1,0:T(8,128)(2,1)}, u32[]{:S(2)}) copy-start(bf16[8,4096]{1,0:T(8,128)(2,1)} %q_ref.1) | copy-start | bytes 196612
  3.5 1.5 %copy-start.7 = (bf16[8,1024]{1,0:T(8,128)(2,1)S(1)}, bf16[8,1024]{1,0:T(8,128)(2,1)}, u32[]{:S(2)}) copy-start(bf16[8,1024]{1,0:T(8,128)(2,1)} %c_ref.1) | copy-start | bytes 49156
  3.5 1.5 %copy-start.8 = (bf16[64,128]{1,0:T(8,128)(2,1)S(1)}, bf16[64,128]{1,0:T(8,128)(2,1)}, u32[]{:S(2)}) copy-start(bf16[64,128]{1,0:T(8,128)(2,1)} %kc_ref.1) | copy-start | bytes 49156
  3.5 1.5 %copy-start.9 = (bf16[64,128]{1,0:T(8,128)(2,1)S(1)}, bf16[64,128]{1,0:T(8,128)(2,1)}, u32[]{:S(2)}) copy-start(bf16[64,128]{1,0:T(8,128)(2,1)} %vc_ref.1) | copy-start | bytes 49156
  4.1 1.0 %copy-start.6 = (bf16[8,1024]{1,0:T(8,128)(2,1)S(1)}, bf16[8,1024]{1,0:T(8,128)(2,1)}, u32[]{:S(2)}) copy-start(bf16[8,1024]{1,0:T(8,128)(2,1)} %b_ref.1) | copy-start | bytes 49156
  4.1 0.9 %copy-start.5 = (bf16[8,1024]{1,0:T(8,128)(2,1)S(1)}, bf16[8,1024]{1,0:T(8,128)(2,1)}, u32[]{:S(2)}) copy-start(bf16[8,1024]{1,0:T(8,128)(2,1)} %v_ref.1) | copy-start | bytes 49156
  4.2 0.8 %copy-start.4 = (bf16[8,1024]{1,0:T(8,128)(2,1)S(1)}, bf16[8,1024]{1,0:T(8,128)(2,1)}, u32[]{:S(2)}) copy-start(bf16[8,1024]{1,0:T(8,128)(2,1)} %k_ref.1) | copy-start | bytes 49156

commit v2 on v1

v2 whole, which is shorter than its diff:
```python
import jax
import jax.numpy as jnp
from jax import lax
from jax.experimental import pallas as pl
from jax.experimental.pallas import tpu as pltpu
from jax.sharding import PartitionSpec as P

Z = 16
LANES = 4
TP = 8
PLANE = LANES * TP
DH = 128
P_SIZE = 64
SPAN = 256
KEYS = 1024
ROWS = 1024
UNIT = 256
REACH = 4
SCALE = 128.0 ** -0.5
LOW = -1e30
MESH = pl.DeviceIdType.MESH
F32 = jnp.float32
BF16 = jnp.bfloat16


def dot(a, b, ca, cb):
    return lax.dot_general(a, b, (((ca,), (cb,)), ((), ())), preferred_element_type=F32)


def in_weights(decay):
    u = 2.0 * decay
    series = 1.0 + u * (1.0 / 12)
    for k in range(11, 1, -1):
        series = 1.0 + u * (1.0 / k) * series
    return jnp.sqrt(jnp.where(u < -1.0, 1.0 - jnp.exp(u), -u * series))


def kernel(
    length_ref, start_ref, skip_ref,
    q_hbm, k_hbm, v_hbm, x_hbm, dec_hbm, b_hbm, c_hbm, kc_hbm, vc_hbm, init_hbm, norm_hbm, gate_hbm,
    attn_ref, ssm_ref,
    q_ref, k_ref, v_ref, x_ref, dec_ref, b_ref, c_ref, kc_ref, vc_ref, init_ref, gain_ref, gate_ref,
    a_send, a_recv, q_send, q_recv, kv_send, kv_recv, g_recv, cache, fresh,
    p1_send, p1_recv, p2_send, p2_recv, p3_send, p3_recv,
    cum_ref, y_ref, o1, m1, l1, o_send, o_recv, y_send, y_recv,
    in_sem, a_ss, a_rs, q_ss, q_rs, kv_ss, kv_rs, g_ss, g_rs, z_ss, z_rs,
    p1_ss, p1_rs, p2_ss, p2_rs, p3_ss, p3_rs, o_ss, o_rs, y_ss, y_rs,
):
    seq, tp = lax.axis_index("seq"), lax.axis_index("tp")
    z, lane = seq // LANES, lax.rem(seq, LANES)
    me = lane * TP + tp
    four, member = z // 4, lax.rem(z, 4)

    loads = [
        pltpu.make_async_copy(src, dst, in_sem.at[n])
        for n, (src, dst) in enumerate(
            (
                (x_hbm, x_ref), (b_hbm, b_ref), (c_hbm, c_ref), (dec_hbm, dec_ref),
                (k_hbm, k_ref), (v_hbm, v_ref), (kc_hbm, kc_ref), (vc_hbm, vc_ref),
                (q_hbm, q_ref), (norm_hbm, gain_ref.at[pl.ds(0, 8)]),
                (init_hbm.at[lane * 4 + member], init_ref), (gate_hbm, gate_ref),
            )
        )
    ]
    for load in loads:
        load.start()
    fresh[...] = jnp.zeros_like(fresh)

    def place(d):
        return (z * LANES + d // TP, lax.rem(d, TP))

    def along(k):
        return (lax.rem(z + Z + k, Z) * LANES + lane, tp)

    barrier = pltpu.get_barrier_semaphore()

    def greet(i, unused):
        pl.semaphore_signal(
            barrier, inc=1, device_id=place(lax.rem(me + i, PLANE)), device_id_type=MESH
        )
        return unused

    offsets = [k for k in range(-REACH, REACH + 1) if k] + [8]
    for k in offsets:
        pl.semaphore_signal(barrier, inc=1, device_id=along(k), device_id_type=MESH)
    lax.fori_loop(1, PLANE, greet, 0)

    for load in loads[:8]:
        load.wait()
    cache[z, 0:64, :] = kc_ref[...]
    cache[z, 64:128, :] = vc_ref[...]
    xx = x_ref[...].astype(F32)
    dec = dec_ref[...].astype(F32)
    bb = b_ref[...].astype(F32)
    cc = c_ref[...].astype(F32)
    kk = k_ref[...].astype(F32)
    vv = v_ref[...].astype(F32)

    def columns(a, first, count):
        return jnp.concatenate(
            [a[:, (first + j) * 128:(first + j + 1) * 128] for j in range(count)], 0
        ).astype(BF16)

    dec_block = jnp.concatenate([dec, dec], 0).astype(BF16)
    for t in range(TP):
        at = slice(t * 128, (t + 1) * 128)
        bc_block = jnp.concatenate([bb[:, at], cc[:, at]], 0).astype(BF16)
        kv_send[t] = jnp.concatenate([kk[:, at], vv[:, at]], 0).astype(BF16)
        for l in range(LANES):
            d = l * TP + t
            a_send[d, 0:16, :] = columns(xx, t * 8 + l * 2, 2)
            a_send[d, 16:32, :] = bc_block
            a_send[d, 32:48, :] = dec_block
    a_recv[me] = a_send[me]
    kv_recv[tp] = kv_send[tp]
    for load in loads[8:10]:
        load.wait()
    qq = q_ref[...].astype(F32)
    for t in range(TP):
        q_send[t] = columns(qq, t * 4, 4)
    q_recv[me] = q_send[tp]
    tile_row = lax.broadcasted_iota(jnp.int32, (8, 128), 0)
    tile_lane = lax.broadcasted_iota(jnp.int32, (8, 128), 1)
    skips = jnp.zeros((8, 128), F32)
    for h in range(16):
        skips = jnp.where(tile_row * 2 + tile_lane // P_SIZE == h, skip_ref[h], skips)
    gain_ref[8:16, :] = skips
    g_recv[tp] = gain_ref[...]
    pl.semaphore_wait(barrier, PLANE - 1 + len(offsets))

    def copy(src, dst, send, recv, device):
        return pltpu.make_async_remote_copy(
            src_ref=src, dst_ref=dst, send_sem=send, recv_sem=recv,
            device_id=device, device_id_type=MESH,
        )

    def kv_copy(t, slot):
        return copy(kv_send.at[t], kv_recv.at[slot], kv_ss.at[t], kv_rs.at[slot], (seq, t))

    def g_copy(t, slot):
        return copy(gain_ref, g_recv.at[slot], g_ss.at[t], g_rs.at[slot], (seq, t))

    def a_copy(d, slot):
        return copy(a_send.at[d], a_recv.at[slot], a_ss.at[d], a_rs.at[slot], place(d))

    def q_copy(d, slot):
        return copy(
            q_send.at[lax.rem(d, TP)], q_recv.at[slot], q_ss.at[d], q_rs.at[slot], place(d)
        )

    def o_copy(d, slot):
        return copy(o_send.at[d], o_recv.at[slot], o_ss.at[d], o_rs.at[slot], place(d))

    def y_copy(d, slot):
        return copy(y_send.at[d], y_recv.at[slot], y_ss.at[d], y_rs.at[slot], place(d))

    def over_plane(act):
        def body(i, unused):
            act(lax.rem(me + i, PLANE))
            return unused

        lax.fori_loop(1, PLANE, body, 0)

    def over_tp(act):
        def body(i, unused):
            act(lax.rem(tp + i, TP))
            return unused

        lax.fori_loop(1, TP, body, 0)

    def hop(buf, ring, from_block, k, mark):
        block = lax.rem(z + Z + from_block, Z)
        return copy(
            buf.at[block], buf.at[block], z_ss.at[ring, mark], z_rs.at[ring, block], along(k)
        )

    def landed(buf, ring, k):
        hop(buf, ring, k, 1, 0).wait_recv()

    def wrapped(k):
        return lax.rem(z + Z + k, Z)

    near = [(0, k, 4 + k, wrapped(k) > z) for k in (4, 3, -3, 2, -2, 1, -1)]
    near.insert(1, (0, -4, 0, z <= 6))
    up_on = [(-4, k, 8 + k, (z >= 4) & (z + k < Z)) for k in (4, 3, 2, 1)]
    down_on = [(4, -k, 12 + k, wrapped(4) <= 3 + k) for k in (3, 2, 1)]
    hops = near + up_on + down_on

    def launch(buf, ring, which, causal):
        for from_block, k, mark, needed in which:
            if causal:
                pl.when(needed)(lambda f=from_block, k=k, m=mark: hop(buf, ring, f, k, m).start())
            else:
                hop(buf, ring, from_block, k, mark).start()

    def arrive(buf, ring, k, causal, also=None):
        if causal:
            needed = wrapped(k) < z
            if also is not None:
                needed = needed | also
            pl.when(needed)(lambda: landed(buf, ring, k))
        else:
            landed(buf, ring, k)

    def sent(buf, ring, causal):
        for from_block, k, mark, needed in hops:
            if causal:
                pl.when(needed)(
                    lambda f=from_block, k=k, m=mark: hop(buf, ring, f, k, m).wait_send()
                )
            else:
                hop(buf, ring, from_block, k, mark).wait_send()

    others = (-1, 1, -2, 2, -3, 3, -5, 5, -6, 6, -7, 7, 8)

    over_tp(lambda t: kv_copy(t, tp).start())
    over_plane(lambda d: a_copy(d, me).start())
    launch(cache, 0, near, False)
    over_plane(lambda d: q_copy(d, me).start())
    over_tp(lambda t: g_copy(t, tp).start())

    arrive(cache, 0, -4, False)
    launch(cache, 0, up_on, False)
    arrive(cache, 0, 4, False)
    launch(cache, 0, down_on, False)

    over_tp(lambda t: kv_copy(t, t).wait_recv())
    kv = kv_recv[...].astype(F32)
    fresh[z, 0:64, :] = kv[:, 0:8, :].reshape(64, DH).astype(BF16)
    fresh[z, 64:128, :] = kv[:, 8:16, :].reshape(64, DH).astype(BF16)
    launch(fresh, 1, near, True)
    over_plane(lambda d: a_copy(d, d).wait_recv())

    def halves(first_row):
        part = a_recv[:, first_row:first_row + 16, :].astype(F32)
        return part[:, 0:8, :].reshape(SPAN, 128), part[:, 8:16, :].reshape(SPAN, 128)

    row = lax.broadcasted_iota(jnp.int32, (SPAN, SPAN), 0)
    col = lax.broadcasted_iota(jnp.int32, (SPAN, SPAN), 1)
    lower = row >= col
    ones = lower.astype(F32).astype(BF16)
    b_all, c_all = halves(16)
    b_all, c_all = b_all.astype(BF16), c_all.astype(BF16)
    mine = (
        lax.broadcasted_iota(jnp.int32, (128, SPAN), 0)
        == tp * 16 + lane * 4 + lax.broadcasted_iota(jnp.int32, (128, SPAN), 1) // P_SIZE
    )
    decay = dot(halves(32)[0].astype(BF16), mine.astype(F32).astype(BF16), 1, 0)
    decay = jnp.where(z * SPAN + row >= start_ref[0], decay, 0.0)
    d_all = decay.astype(BF16)
    x_all = jnp.concatenate(halves(0), 1) * in_weights(decay)
    cum = dot(ones, d_all, 1, 0)
    end = cum[SPAN - 1:SPAN, :]
    local = dot((x_all * jnp.exp(end - cum)).astype(BF16), b_all, 0, 0).astype(BF16)

    def log_rows(log):
        high = log.astype(BF16).astype(F32)
        return jnp.concatenate(
            [jnp.broadcast_to(high, (8, 128)), jnp.broadcast_to(log - high, (8, 128))], 0
        ).astype(BF16)

    for h in range(4):
        p1_send[h, 0:64, :] = local[h * P_SIZE:(h + 1) * P_SIZE, :]
        p1_send[h, 64:80, :] = log_rows(
            jnp.broadcast_to(end[:, h * P_SIZE:h * P_SIZE + 1], (1, 128))
        )
    p1_recv[member] = p1_send[member]

    def peer(k):
        return lax.rem(member + k, 4)

    def in_four(m):
        return ((four * 4 + m) * LANES + lane, tp)

    def p1_copy(m, slot):
        return copy(p1_send.at[m], p1_recv.at[slot], p1_ss.at[m], p1_rs.at[slot], in_four(m))

    def p2_copy(f, slot):
        return copy(
            p2_send, p2_recv.at[slot], p2_ss.at[f], p2_rs.at[slot],
            ((f * 4 + member) * LANES + lane, tp),
        )

    def p3_copy(m, slot):
        return copy(p3_send.at[m], p3_recv.at[slot], p3_ss.at[m], p3_rs.at[slot], in_four(m))

    for k in (1, 2, 3):
        p1_copy(peer(k), member).start()
    cum_ref[...] = cum

    x_all = x_all.astype(BF16)
    cum_t = dot(d_all, ones, 0, 1)
    pair = dot(c_all, b_all, 1, 1)
    first_half = lax.broadcasted_iota(jnp.int32, (SPAN, 128), 1) < P_SIZE
    for half in range(2):
        parts = []
        for j in (2 * half, 2 * half + 1):
            gap = cum[:, j * P_SIZE:j * P_SIZE + 1] - cum_t[j * P_SIZE:j * P_SIZE + 1, :]
            fade = jnp.where(lower, jnp.exp(jnp.where(lower, gap, 0.0)), 0.0)
            parts.append(
                dot((pair * fade).astype(BF16), x_all[:, half * 128:(half + 1) * 128], 1, 0)
            )
        y_ref[:, half * 128:(half + 1) * 128] = jnp.where(first_half, parts[0], parts[1])

    arrive(fresh, 1, -4, True)
    launch(fresh, 1, up_on, True)
    arrive(fresh, 1, 4, True, wrapped(4) <= 6)
    launch(fresh, 1, down_on, True)

    for k in (1, 2, 3):
        p1_copy(peer(k), peer(k)).wait_recv()

    def state_of(tile):
        tail = tile[64:80, :].astype(F32)
        return tile[0:64, :].astype(F32), tail[0:1, :] + tail[8:9, :]

    steps = [state_of(p1_recv[m]) for m in range(4)]
    total, total_log = steps[0]
    for add, log in steps[1:]:
        total, total_log = total * jnp.exp(log) + add, total_log + log
    p2_send[0:64, :] = total.astype(BF16)
    p2_send[64:80, :] = log_rows(total_log)
    for k in (1, 2, 3):
        pl.when(four + k < 4)(lambda k=k: p2_copy(four + k, four).start())

    key_at = lax.broadcasted_iota(jnp.int32, (1, KEYS), 1)
    key_place = (key_at // 64) * SPAN + lane * 64 + lax.rem(key_at, 64)
    row_at = lax.broadcasted_iota(jnp.int32, (UNIT, 1), 0)

    def part(u, buf, usable):
        queries = q_recv[pl.ds(u * 8, 8)].reshape(UNIT, DH)
        keys = buf[:, 0:64, :].reshape(KEYS, DH)
        values = buf[:, 64:128, :].reshape(KEYS, DH)
        scores = jnp.where(usable, dot(queries, keys, 1, 1) * SCALE, LOW)
        top = jnp.max(scores, axis=1, keepdims=True)
        weights = jnp.exp(scores - top)
        total = jnp.sum(weights, axis=1, keepdims=True)
        return top, total, dot(weights.astype(BF16), values, 1, 0)

    over_plane(lambda d: q_copy(d, d).wait_recv())
    for k in others:
        arrive(cache, 0, k, False)
    cached = key_place < length_ref[0]
    for u in range(ROWS // UNIT):
        top, weight, mixed = part(u, cache, cached)
        m1[u * UNIT:(u + 1) * UNIT, :] = top
        l1[u * UNIT:(u + 1) * UNIT, :] = weight
        o1[u * UNIT:(u + 1) * UNIT, :] = mixed

    loads[10].wait()
    for k in (1, 2, 3):
        pl.when(four - k >= 0)(lambda k=k: p2_copy(four, four - k).wait_recv())

    def lap(f, prior):
        add, log = state_of(p2_recv[f])
        return prior * jnp.exp(log) + add

    prior = lax.fori_loop(0, four, lap, init_ref[...])
    for m in range(4):
        p3_send[m] = prior.astype(BF16)
        if m < 3:
            prior = prior * jnp.exp(steps[m][1]) + steps[m][0]
    p3_recv[member] = p3_send[member]
    for k in (1, 2, 3):
        p3_copy(peer(k), member).start()

    for k in others:
        arrive(fresh, 1, k, True)
    spot = (
        lax.broadcasted_iota(jnp.int32, (1, 32, 128), 1)
        == lax.broadcasted_iota(jnp.int32, (1, 32, 128), 2)
    ).astype(F32)
    spot_row = lax.broadcasted_iota(jnp.int32, (8, 16, 128), 1)
    for u in range(ROWS // UNIT):
        query_place = z * SPAN + u * 64 + (row_at // 32) * 8 + lax.rem(row_at, 8)
        usable = (key_place >= start_ref[0]) & (key_place <= query_place)
        top, weight, mixed = part(u, fresh, usable)
        top1, weight1 = m1[u * UNIT:(u + 1) * UNIT, :], l1[u * UNIT:(u + 1) * UNIT, :]
        both = jnp.maximum(top, top1)
        by, by1 = jnp.exp(top - both), jnp.exp(top1 - both)
        weight = weight * by + weight1 * by1
        mixed = (mixed * by + o1[u * UNIT:(u + 1) * UNIT, :] * by1) / weight
        o_send[u * 8:(u + 1) * 8, 0:32, :] = mixed.astype(BF16).reshape(8, 32, DH)
        size = jnp.broadcast_to(both + jnp.log(weight), (UNIT, 128)).reshape(8, 32, 128)
        size = jnp.sum(size * spot, axis=1, keepdims=True)
        high = size.astype(BF16).astype(F32)
        middle = (size - high).astype(BF16).astype(F32)
        o_send[u * 8:(u + 1) * 8, 32:48, :] = jnp.where(
            spot_row < 8, high, jnp.where(spot_row < 15, middle, size - high - middle)
        ).astype(BF16)
    o_recv[me] = o_send[me]
    over_plane(lambda d: o_copy(d, me).start())

    for k in (1, 2, 3):
        p3_copy(peer(k), peer(k)).wait_recv()
    incoming = p3_recv[...].reshape(SPAN, 128)
    y = y_ref[...] + jnp.exp(cum_ref[...]) * dot(c_all, incoming, 1, 1)
    y_send[...] = jnp.concatenate(
        [y[:, 0:128].reshape(PLANE, 8, 128), y[:, 128:256].reshape(PLANE, 8, 128)], 1
    ).astype(BF16)
    y_recv[me] = y_send[me]
    over_plane(lambda d: y_copy(d, me).start())

    over_plane(lambda d: o_copy(d, d).wait_recv())
    for t in range(TP):
        sizes = []
        for l in range(LANES):
            tile = o_recv[l * TP + t, 32:48, :].astype(F32)
            line = tile[0:1, :] + tile[8:9, :] + tile[15:16, :]
            sizes.append(jnp.sum(line * spot[0], axis=1, keepdims=True))
        most = jnp.maximum(jnp.maximum(sizes[0], sizes[1]), jnp.maximum(sizes[2], sizes[3]))
        shares = [jnp.exp(size - most) for size in sizes]
        whole = shares[0] + shares[1] + shares[2] + shares[3]
        out = sum(
            share * o_recv[l * TP + t, 0:32, :].astype(F32) for l, share in enumerate(shares)
        ) / whole
        for h in range(4):
            at = (t * 4 + h) * 128
            attn_ref[:, at:at + 128] = out[h * 8:(h + 1) * 8, :].astype(BF16)

    over_tp(lambda t: g_copy(t, t).wait_recv())
    loads[11].wait()
    over_plane(lambda d: y_copy(d, d).wait_recv())
    for t in range(TP):
        gated, squares = [], 0.0
        for l in range(LANES):
            y_part = y_recv[l * TP + t].astype(F32)
            for half in range(2):
                r = l * 2 + half
                at = t * 1024 + r * 128
                gate = gate_ref[:, at:at + 128].astype(F32)
                value = y_part[half * 8:(half + 1) * 8, :] + g_recv[
                    t, 8 + r:9 + r, :
                ] * x_ref[:, at:at + 128].astype(F32)
                value = value * (gate / (1.0 + jnp.exp(-gate)))
                squares = squares + value * value
                gated.append(value)
        scale = lax.rsqrt(jnp.sum(squares, axis=1, keepdims=True) * (1.0 / 1024) + 1e-5)
        for r in range(8):
            at = t * 1024 + r * 128
            ssm_ref[:, at:at + 128] = (gated[r] * scale * g_recv[t, r:r + 1, :]).astype(BF16)

    over_tp(lambda t: kv_copy(t, tp).wait_send())
    over_tp(lambda t: g_copy(t, tp).wait_send())
    over_plane(lambda d: a_copy(d, me).wait_send())
    over_plane(lambda d: q_copy(d, me).wait_send())
    over_plane(lambda d: o_copy(d, me).wait_send())
    over_plane(lambda d: y_copy(d, me).wait_send())
    sent(cache, 0, False)
    sent(fresh, 1, True)
    for k in (1, 2, 3):
        p1_copy(peer(k), member).wait_send()
        pl.when(four + k < 4)(lambda k=k: p2_copy(four + k, four).wait_send())
        p3_copy(peer(k), member).wait_send()


def local(
    query, key_new, value_new, ssm_input, ssm_gate, ssm_b, ssm_c, log_decay,
    key_cache, value_cache, init_state, skip_gain, norm_gain, cache_length, span_start,
):
    vmem = pl.BlockSpec(memory_space=pltpu.VMEM)
    smem = pl.BlockSpec(memory_space=pltpu.SMEM)
    hbm = pl.BlockSpec(memory_space=pltpu.HBM)
    dma = pltpu.SemaphoreType.DMA
    return pl.pallas_call(
        kernel,
        out_shape=(
            jax.ShapeDtypeStruct((8, 4096), BF16),
            jax.ShapeDtypeStruct((8, 8192), BF16),
        ),
        in_specs=[smem] * 3 + [hbm] * 12,
        out_specs=(vmem, vmem),
        scratch_shapes=[
            pltpu.VMEM((8, 4096), BF16),
            pltpu.VMEM((8, 1024), BF16),
            pltpu.VMEM((8, 1024), BF16),
            pltpu.VMEM((8, 8192), BF16),
            pltpu.VMEM((8, 128), BF16),
            pltpu.VMEM((8, 1024), BF16),
            pltpu.VMEM((8, 1024), BF16),
            pltpu.VMEM((64, 128), BF16),
            pltpu.VMEM((64, 128), BF16),
            pltpu.VMEM((64, 128), F32),
            pltpu.VMEM((16, 128), F32),
            pltpu.VMEM((8, 8192), BF16),
            pltpu.VMEM((PLANE, 48, 128), BF16),
            pltpu.VMEM((PLANE, 48, 128), BF16),
            pltpu.VMEM((TP, 32, 128), BF16),
            pltpu.VMEM((PLANE, 32, 128), BF16),
            pltpu.VMEM((TP, 16, 128), BF16),
            pltpu.VMEM((TP, 16, 128), BF16),
            pltpu.VMEM((TP, 16, 128), F32),
            pltpu.VMEM((Z, 128, DH), BF16),
            pltpu.VMEM((Z, 128, DH), BF16),
            pltpu.VMEM((4, 80, 128), BF16),
            pltpu.VMEM((4, 80, 128), BF16),
            pltpu.VMEM((80, 128), BF16),
            pltpu.VMEM((4, 80, 128), BF16),
            pltpu.VMEM((4, 64, 128), BF16),
            pltpu.VMEM((4, 64, 128), BF16),
            pltpu.VMEM((SPAN, SPAN), F32),
            pltpu.VMEM((SPAN, SPAN), F32),
            pltpu.VMEM((ROWS, DH), F32),
            pltpu.VMEM((ROWS, 1), F32),
            pltpu.VMEM((ROWS, 1), F32),
            pltpu.VMEM((PLANE, 48, 128), BF16),
            pltpu.VMEM((PLANE, 48, 128), BF16),
            pltpu.VMEM((PLANE, 16, 128), BF16),
            pltpu.VMEM((PLANE, 16, 128), BF16),
            dma((12,)),
            dma((PLANE,)), dma((PLANE,)),
            dma((PLANE,)), dma((PLANE,)),
            dma((TP,)), dma((TP,)),
            dma((TP,)), dma((TP,)),
            dma((2, 16)), dma((2, Z)),
            dma((4,)), dma((4,)),
            dma((4,)), dma((4,)),
            dma((4,)), dma((4,)),
            dma((PLANE,)), dma((PLANE,)),
            dma((PLANE,)), dma((PLANE,)),
        ],
        compiler_params=pltpu.CompilerParams(
            collective_id=0, has_side_effects=True, vmem_limit_bytes=56 * 1024 * 1024
        ),
        name="mixers",
    )(
        cache_length, span_start, skip_gain,
        query, key_new, value_new, ssm_input, log_decay, ssm_b, ssm_c,
        key_cache, value_cache, init_state, norm_gain.reshape(8, 128), ssm_gate,
    )


def solution(mesh):
    rows = P(("seq", "tp"), None)
    placed = (rows,) * 8 + (
        P("seq", "tp"),
        P("seq", "tp"),
        P("tp", None, None),
        P("tp"),
        P("tp"),
        P(),
        P(),
    )
    return jax.shard_map(
        local, mesh=mesh, in_specs=placed, out_specs=(rows, rows), check_vma=False
    )
```

time: 80.6 us -> 70.9 us (0.88)
  the two profiles are of different devices: /device:TPU:1 before, /device:TPU:448 now
where the time goes in v2:
time: 70.9 us; the launch traced here: 70.7 us
  Pallas kernels  66.6 us (94%)
  local copies, waits for them, and re-layouts  2.17 us (3%)
  between operations  1.94 us (3%)
    pallas_call x1, Pallas kernels, local(): pl.pallas_call(kernel, out_shape=(jax.ShapeDtypeStruct((8, 4096), BF16),...  66.6 us
    unnamed x4, local copies, waits for them, and re-layouts  2.17 us

profile of v2, /device:TPU:448, one launch (start us, length us, event | category | flops | bytes accessed | tf_op | source)
XLA Modules:
  0.0 70.7 jit_solution(14515419714501538639)
XLA Ops:
  1.9 66.6 %mixers.1 = (bf16[8,4096]{1,0:T(8,128)(2,1)}, bf16[8,8192]{1,0:T(8,128)(2,1)}) custom-call(s32[1]{0:T(128)S(6)} %copy.19.length_ref, s32[1]{0:T(128)S(6)} %copy.20.start_ref, f32[16]{0:T(128)} %skip_ref.1, bf16[8,4096]{1,0:T(8,128)(2,1)} %q_hbm.1, bf16[8,1024]{1,0:T(8,128)(2,1)} %k_hbm.1, bf16[8,1024]{1,0:T(8,128)(2,1)} %v_hbm.1, bf16[8,8192]{1,0:T(8,128)(2,1)} %x_hbm.1, ...), custom_call_target="tpu_custom_call" | custom-call | tf_op jit(solution)/shard_map/mixers/pallas_call | solution.py:465
  68.5 0.0 copy-start
  68.6 1.5 %copy.21 = bf16[8,4096]{1,0:T(8,128)(2,1)} copy(bf16[8,4096]{1,0:T(8,128)(2,1)} %get-tuple-element.4) | data formatting | bytes 131072
  70.1 0.0 copy-done
  70.1 0.7 copy.22
Async XLA Ops:
  68.5 1.5 %copy-start = (bf16[8,8192]{1,0:T(8,128)(2,1)S(1)}, bf16[8,8192]{1,0:T(8,128)(2,1)}, u32[]{:S(2)}) copy-start(bf16[8,8192]{1,0:T(8,128)(2,1)} %get-tuple-element.5) | copy-start | bytes 393220

commit v3 on v2

--- a/solution.py
+++ b/solution.py
@@ -16,6 +16,7 @@
 ROWS = 1024
 UNIT = 256
 REACH = 4
+ROUNDS = 4
 SCALE = 128.0 ** -0.5
 LOW = -1e30
 MESH = pl.DeviceIdType.MESH
@@ -43,8 +44,7 @@
     a_send, a_recv, q_send, q_recv, kv_send, kv_recv, g_recv, cache, fresh,
     p1_send, p1_recv, p2_send, p2_recv, p3_send, p3_recv,
     cum_ref, y_ref, o1, m1, l1, o_send, o_recv, y_send, y_recv,
-    in_sem, a_ss, a_rs, q_ss, q_rs, kv_ss, kv_rs, g_ss, g_rs, z_ss, z_rs,
-    p1_ss, p1_rs, p2_ss, p2_rs, p3_ss, p3_rs, o_ss, o_rs, y_ss, y_rs,
+    in_sem, a_sem, q_sem, kv_sem, g_sem, z_ss, z_rs, p1_sem, p2_ss, p2_rs, p3_sem, o_sem, y_sem,
 ):
     seq, tp = lax.axis_index("seq"), lax.axis_index("tp")
     z, lane = seq // LANES, lax.rem(seq, LANES)
@@ -135,24 +135,28 @@
         )
 
     def kv_copy(t, slot):
-        return copy(kv_send.at[t], kv_recv.at[slot], kv_ss.at[t], kv_rs.at[slot], (seq, t))
+        return copy(kv_send.at[t], kv_recv.at[slot], kv_sem.at[0], kv_sem.at[1], (seq, t))
 
     def g_copy(t, slot):
-        return copy(gain_ref, g_recv.at[slot], g_ss.at[t], g_rs.at[slot], (seq, t))
+        return copy(gain_ref, g_recv.at[slot], g_sem.at[0], g_sem.at[1], (seq, t))
 
     def a_copy(d, slot):
-        return copy(a_send.at[d], a_recv.at[slot], a_ss.at[d], a_rs.at[slot], place(d))
+        return copy(a_send.at[d], a_recv.at[slot], a_sem.at[0], a_sem.at[1], place(d))
 
     def q_copy(d, slot):
         return copy(
-            q_send.at[lax.rem(d, TP)], q_recv.at[slot], q_ss.at[d], q_rs.at[slot], place(d)
+            q_send.at[lax.rem(d, TP)], q_recv.at[slot], q_sem.at[0], q_sem.at[1], place(d)
         )
 
     def o_copy(d, slot):
-        return copy(o_send.at[d], o_recv.at[slot], o_ss.at[d], o_rs.at[slot], place(d))
+        return copy(o_send.at[d], o_recv.at[slot], o_sem.at[0], o_sem.at[1], place(d))
 
     def y_copy(d, slot):
-        return copy(y_send.at[d], y_recv.at[slot], y_ss.at[d], y_rs.at[slot], place(d))
+        return copy(y_send.at[d], y_recv.at[slot], y_sem.at[0], y_sem.at[1], place(d))
+
+    def settle(buf, sem, count):
+        part = buf.at[pl.ds(0, count)]
+        pltpu.make_async_copy(part, part, sem).wait()
 
     def over_plane(act):
         def body(i, unused):
@@ -180,11 +184,17 @@
     def wrapped(k):
         return lax.rem(z + Z + k, Z)
 
-    near = [(0, k, 4 + k, wrapped(k) > z) for k in (4, 3, -3, 2, -2, 1, -1)]
-    near.insert(1, (0, -4, 0, z <= 6))
-    up_on = [(-4, k, 8 + k, (z >= 4) & (z + k < Z)) for k in (4, 3, 2, 1)]
-    down_on = [(4, -k, 12 + k, wrapped(4) <= 3 + k) for k in (3, 2, 1)]
-    hops = near + up_on + down_on
+    def ups(r):
+        return [(-2 * r, k, 2 * r + k - 1, (z >= 2 * r) & (z + k < Z)) for k in (2, 1)]
+
+    def downs(r):
+        block = wrapped(2 * r)
+        return [
+            (2 * r, -k, 7 + 2 * r + k, block <= (6 if k == 2 else 2 * r))
+            for k in ((2, 1) if r < ROUNDS - 1 else (1,))
+        ]
+
+    hops = [one for r in range(ROUNDS) for one in ups(r) + downs(r)]
 
     def launch(buf, ring, which, causal):
         for from_block, k, mark, needed in which:
@@ -193,14 +203,21 @@
             else:
                 hop(buf, ring, from_block, k, mark).start()
 
-    def arrive(buf, ring, k, causal, also=None):
+    def arrive(buf, ring, k, causal):
         if causal:
-            needed = wrapped(k) < z
-            if also is not None:
-                needed = needed | also
-            pl.when(needed)(lambda: landed(buf, ring, k))
+            block = wrapped(k)
+            pl.when(block <= 6 if k in (2, 4, 6) else block < z)(lambda: landed(buf, ring, k))
         else:
             landed(buf, ring, k)
+
+    def begin(buf, ring, causal):
+        launch(buf, ring, ups(0) + downs(0), causal)
+
+    def forward(buf, ring, r, causal):
+        arrive(buf, ring, -2 * r, causal)
+        launch(buf, ring, ups(r), causal)
+        arrive(buf, ring, 2 * r, causal)
+        launch(buf, ring, downs(r), causal)
 
     def sent(buf, ring, causal):
         for from_block, k, mark, needed in hops:
@@ -211,25 +228,24 @@
             else:
                 hop(buf, ring, from_block, k, mark).wait_send()
 
-    others = (-1, 1, -2, 2, -3, 3, -5, 5, -6, 6, -7, 7, 8)
+    others = (-1, 1, -3, 3, -5, 5, -7, 7, 8)
 
     over_tp(lambda t: kv_copy(t, tp).start())
     over_plane(lambda d: a_copy(d, me).start())
-    launch(cache, 0, near, False)
+    begin(cache, 0, False)
     over_plane(lambda d: q_copy(d, me).start())
     over_tp(lambda t: g_copy(t, tp).start())
 
-    arrive(cache, 0, -4, False)
-    launch(cache, 0, up_on, False)
-    arrive(cache, 0, 4, False)
-    launch(cache, 0, down_on, False)
-
-    over_tp(lambda t: kv_copy(t, t).wait_recv())
+    forward(cache, 0, 1, False)
+
+    settle(kv_recv, kv_sem.at[1], TP - 1)
     kv = kv_recv[...].astype(F32)
     fresh[z, 0:64, :] = kv[:, 0:8, :].reshape(64, DH).astype(BF16)
     fresh[z, 64:128, :] = kv[:, 8:16, :].reshape(64, DH).astype(BF16)
-    launch(fresh, 1, near, True)
-    over_plane(lambda d: a_copy(d, d).wait_recv())
+    begin(fresh, 1, True)
+    forward(cache, 0, 2, False)
+    settle(a_recv, a_sem.at[1], PLANE - 1)
+    forward(fresh, 1, 1, True)
 
     def halves(first_row):
         part = a_recv[:, first_row:first_row + 16, :].astype(F32)
@@ -273,7 +289,7 @@
         return ((four * 4 + m) * LANES + lane, tp)
 
     def p1_copy(m, slot):
-        return copy(p1_send.at[m], p1_recv.at[slot], p1_ss.at[m], p1_rs.at[slot], in_four(m))
+        return copy(p1_send.at[m], p1_recv.at[slot], p1_sem.at[0], p1_sem.at[1], in_four(m))
 
     def p2_copy(f, slot):
         return copy(
@@ -282,11 +298,12 @@
         )
 
     def p3_copy(m, slot):
-        return copy(p3_send.at[m], p3_recv.at[slot], p3_ss.at[m], p3_rs.at[slot], in_four(m))
+        return copy(p3_send.at[m], p3_recv.at[slot], p3_sem.at[0], p3_sem.at[1], in_four(m))
 
     for k in (1, 2, 3):
         p1_copy(peer(k), member).start()
     cum_ref[...] = cum
+    forward(cache, 0, 3, False)
 
     x_all = x_all.astype(BF16)
     cum_t = dot(d_all, ones, 0, 1)
@@ -302,13 +319,9 @@
             )
         y_ref[:, half * 128:(half + 1) * 128] = jnp.where(first_half, parts[0], parts[1])
 
-    arrive(fresh, 1, -4, True)
-    launch(fresh, 1, up_on, True)
-    arrive(fresh, 1, 4, True, wrapped(4) <= 6)
-    launch(fresh, 1, down_on, True)
-
-    for k in (1, 2, 3):
-        p1_copy(peer(k), peer(k)).wait_recv()
+    forward(fresh, 1, 2, True)
+
+    settle(p1_recv, p1_sem.at[1], 3)
 
     def state_of(tile):
         tail = tile[64:80, :].astype(F32)
@@ -322,6 +335,28 @@
     p2_send[64:80, :] = log_rows(total_log)
     for k in (1, 2, 3):
         pl.when(four + k < 4)(lambda k=k: p2_copy(four + k, four).start())
+
+    def spread():
+        for k in (1, 2, 3):
+            pl.when(four - k >= 0)(lambda k=k: p2_copy(four, four - k).wait_recv())
+
+        def lap(f, prior):
+            add, log = state_of(p2_recv[f])
+            return prior * jnp.exp(log) + add
+
+        prior = lax.fori_loop(0, four, lap, init_ref[...])
+        for m in range(4):
+            p3_send[m] = prior.astype(BF16)
+            if m < 3:
+                add, log = state_of(p1_recv[m])
+                prior = prior * jnp.exp(log) + add
+        p3_recv[member] = p3_send[member]
+        for k in (1, 2, 3):
+            p3_copy(peer(k), member).start()
+
+    loads[10].wait()
+    pl.when(four == 0)(spread)
+    forward(fresh, 1, 3, True)
 
     key_at = lax.broadcasted_iota(jnp.int32, (1, KEYS), 1)
     key_place = (key_at // 64) * SPAN + lane * 64 + lax.rem(key_at, 64)
@@ -337,7 +372,7 @@
         total = jnp.sum(weights, axis=1, keepdims=True)
         return top, total, dot(weights.astype(BF16), values, 1, 0)
 
-    over_plane(lambda d: q_copy(d, d).wait_recv())
+    settle(q_recv, q_sem.at[1], PLANE - 1)
     for k in others:
         arrive(cache, 0, k, False)
     cached = key_place < length_ref[0]
@@ -347,22 +382,7 @@
         l1[u * UNIT:(u + 1) * UNIT, :] = weight
         o1[u * UNIT:(u + 1) * UNIT, :] = mixed
 
-    loads[10].wait()
-    for k in (1, 2, 3):
-        pl.when(four - k >= 0)(lambda k=k: p2_copy(four, four - k).wait_recv())
-
-    def lap(f, prior):
-        add, log = state_of(p2_recv[f])
-        return prior * jnp.exp(log) + add
-
-    prior = lax.fori_loop(0, four, lap, init_ref[...])
-    for m in range(4):
-        p3_send[m] = prior.astype(BF16)
-        if m < 3:
-            prior = prior * jnp.exp(steps[m][1]) + steps[m][0]
-    p3_recv[member] = p3_send[member]
-    for k in (1, 2, 3):
-        p3_copy(peer(k), member).start()
+    pl.when(four > 0)(spread)
 
     for k in others:
         arrive(fresh, 1, k, True)
@@ -371,28 +391,36 @@
         == lax.broadcasted_iota(jnp.int32, (1, 32, 128), 2)
     ).astype(F32)
     spot_row = lax.broadcasted_iota(jnp.int32, (8, 16, 128), 1)
-    for u in range(ROWS // UNIT):
+
+    def unit(i, unused):
+        u = lax.rem(lane + 1 + i, LANES)
         query_place = z * SPAN + u * 64 + (row_at // 32) * 8 + lax.rem(row_at, 8)
         usable = (key_place >= start_ref[0]) & (key_place <= query_place)
         top, weight, mixed = part(u, fresh, usable)
-        top1, weight1 = m1[u * UNIT:(u + 1) * UNIT, :], l1[u * UNIT:(u + 1) * UNIT, :]
+        rows = pl.ds(pl.multiple_of(u * UNIT, UNIT), UNIT)
+        top1, weight1 = m1[rows, :], l1[rows, :]
         both = jnp.maximum(top, top1)
         by, by1 = jnp.exp(top - both), jnp.exp(top1 - both)
         weight = weight * by + weight1 * by1
-        mixed = (mixed * by + o1[u * UNIT:(u + 1) * UNIT, :] * by1) / weight
-        o_send[u * 8:(u + 1) * 8, 0:32, :] = mixed.astype(BF16).reshape(8, 32, DH)
+        mixed = (mixed * by + o1[rows, :] * by1) / weight
+        o_send[pl.ds(u * 8, 8), 0:32, :] = mixed.astype(BF16).reshape(8, 32, DH)
         size = jnp.broadcast_to(both + jnp.log(weight), (UNIT, 128)).reshape(8, 32, 128)
         size = jnp.sum(size * spot, axis=1, keepdims=True)
         high = size.astype(BF16).astype(F32)
         middle = (size - high).astype(BF16).astype(F32)
-        o_send[u * 8:(u + 1) * 8, 32:48, :] = jnp.where(
+        o_send[pl.ds(u * 8, 8), 32:48, :] = jnp.where(
             spot_row < 8, high, jnp.where(spot_row < 15, middle, size - high - middle)
         ).astype(BF16)
+        for n in range(1, TP):
+            o_copy(u * TP + lax.rem(tp + n, TP), me).start()
+        pl.when(u != lane)(lambda: o_copy(u * TP + tp, me).start())
+        return unused
+
+    for i in range(LANES):
+        unit(i, 0)
     o_recv[me] = o_send[me]
-    over_plane(lambda d: o_copy(d, me).start())
-
-    for k in (1, 2, 3):
-        p3_copy(peer(k), peer(k)).wait_recv()
+
+    settle(p3_recv, p3_sem.at[1], 3)
     incoming = p3_recv[...].reshape(SPAN, 128)
     y = y_ref[...] + jnp.exp(cum_ref[...]) * dot(c_all, incoming, 1, 1)
     y_send[...] = jnp.concatenate(
@@ -401,7 +429,7 @@
     y_recv[me] = y_send[me]
     over_plane(lambda d: y_copy(d, me).start())
 
-    over_plane(lambda d: o_copy(d, d).wait_recv())
+    settle(o_recv, o_sem.at[1], PLANE - 1)
     for t in range(TP):
         sizes = []
         for l in range(LANES):
@@ -418,9 +446,9 @@
             at = (t * 4 + h) * 128
             attn_ref[:, at:at + 128] = out[h * 8:(h + 1) * 8, :].astype(BF16)
 
-    over_tp(lambda t: g_copy(t, t).wait_recv())
+    settle(g_recv, g_sem.at[1], TP - 1)
     loads[11].wait()
-    over_plane(lambda d: y_copy(d, d).wait_recv())
+    settle(y_recv, y_sem.at[1], PLANE - 1)
     for t in range(TP):
         gated, squares = [], 0.0
         for l in range(LANES):
@@ -440,18 +468,18 @@
             at = t * 1024 + r * 128
             ssm_ref[:, at:at + 128] = (gated[r] * scale * g_recv[t, r:r + 1, :]).astype(BF16)
 
-    over_tp(lambda t: kv_copy(t, tp).wait_send())
-    over_tp(lambda t: g_copy(t, tp).wait_send())
-    over_plane(lambda d: a_copy(d, me).wait_send())
-    over_plane(lambda d: q_copy(d, me).wait_send())
-    over_plane(lambda d: o_copy(d, me).wait_send())
-    over_plane(lambda d: y_copy(d, me).wait_send())
+    settle(kv_recv, kv_sem.at[0], TP - 1)
+    settle(g_recv, g_sem.at[0], TP - 1)
+    settle(a_recv, a_sem.at[0], PLANE - 1)
+    settle(q_recv, q_sem.at[0], PLANE - 1)
+    settle(o_recv, o_sem.at[0], PLANE - 1)
+    settle(y_recv, y_sem.at[0], PLANE - 1)
+    settle(p1_recv, p1_sem.at[0], 3)
+    settle(p3_recv, p3_sem.at[0], 3)
     sent(cache, 0, False)
     sent(fresh, 1, True)
     for k in (1, 2, 3):
-        p1_copy(peer(k), member).wait_send()
         pl.when(four + k < 4)(lambda k=k: p2_copy(four + k, four).wait_send())
-        p3_copy(peer(k), member).wait_send()
 
 
 def local(
@@ -507,17 +535,9 @@
             pltpu.VMEM((PLANE, 48, 128), BF16),
             pltpu.VMEM((PLANE, 16, 128), BF16),
             pltpu.VMEM((PLANE, 16, 128), BF16),
-            dma((12,)),
-            dma((PLANE,)), dma((PLANE,)),
-            dma((PLANE,)), dma((PLANE,)),
-            dma((TP,)), dma((TP,)),
-            dma((TP,)), dma((TP,)),
+            dma((12,)), dma((2,)), dma((2,)), dma((2,)), dma((2,)),
             dma((2, 16)), dma((2, Z)),
-            dma((4,)), dma((4,)),
-            dma((4,)), dma((4,)),
-            dma((4,)), dma((4,)),
-            dma((PLANE,)), dma((PLANE,)),
-            dma((PLANE,)), dma((PLANE,)),
+            dma((2,)), dma((4,)), dma((4,)), dma((2,)), dma((2,)), dma((2,)),
         ],
         compiler_params=pltpu.CompilerParams(
             collective_id=0, has_side_effects=True, vmem_limit_bytes=56 * 1024 * 1024

time: 70.9 us -> 54.8 us (0.77)
  the two profiles are of different devices: /device:TPU:448 before, /device:TPU:1 now
where the time goes in v3:
time: 54.8 us; the launch traced here: 54.6 us
  Pallas kernels  50.5 us (92%)
  local copies, waits for them, and re-layouts  2.17 us (4%)
  between operations  1.94 us (4%)
    pallas_call x1, Pallas kernels, local(): pl.pallas_call(kernel, out_shape=(jax.ShapeDtypeStruct((8, 4096), BF16),...  50.5 us
    unnamed x4, local copies, waits for them, and re-layouts  2.17 us

profile of v3, /device:TPU:1, one launch (start us, length us, event | category | flops | bytes accessed | tf_op | source)
XLA Modules:
  0.0 54.6 jit_solution(7237383558834721054)
XLA Ops:
  1.9 50.5 %mixers.1 = (bf16[8,4096]{1,0:T(8,128)(2,1)}, bf16[8,8192]{1,0:T(8,128)(2,1)}) custom-call(s32[1]{0:T(128)S(6)} %copy.19.length_ref, s32[1]{0:T(128)S(6)} %copy.20.start_ref, f32[16]{0:T(128)} %skip_ref.1, bf16[8,4096]{1,0:T(8,128)(2,1)} %q_hbm.1, bf16[8,1024]{1,0:T(8,128)(2,1)} %k_hbm.1, bf16[8,1024]{1,0:T(8,128)(2,1)} %v_hbm.1, bf16[8,8192]{1,0:T(8,128)(2,1)} %x_hbm.1, ...), custom_call_target="tpu_custom_call" | custom-call | tf_op jit(solution)/shard_map/mixers/pallas_call | solution.py:493
  52.4 0.0 copy-start
  52.4 1.5 %copy.21 = bf16[8,4096]{1,0:T(8,128)(2,1)} copy(bf16[8,4096]{1,0:T(8,128)(2,1)} %get-tuple-element.4) | data formatting | bytes 131072
  54.0 0.0 copy-done
  54.0 0.7 %copy.22 = bf16[8,8192]{1,0:T(8,128)(2,1)} copy(bf16[8,8192]{1,0:T(8,128)(2,1)S(1)} %copy-done) | data formatting | bytes 262144
Async XLA Ops:
  52.4 1.5 %copy-start = (bf16[8,8192]{1,0:T(8,128)(2,1)S(1)}, bf16[8,8192]{1,0:T(8,128)(2,1)}, u32[]{:S(2)}) copy-start(bf16[8,8192]{1,0:T(8,128)(2,1)} %get-tuple-element.5) | copy-start | bytes 393220

commit v4 on v3

--- a/solution.py
+++ b/solution.py
@@ -43,7 +43,7 @@
     q_ref, k_ref, v_ref, x_ref, dec_ref, b_ref, c_ref, kc_ref, vc_ref, init_ref, gain_ref, gate_ref,
     a_send, a_recv, q_send, q_recv, kv_send, kv_recv, g_recv, cache, fresh,
     p1_send, p1_recv, p2_send, p2_recv, p3_send, p3_recv,
-    cum_ref, y_ref, o1, m1, l1, o_send, o_recv, y_send, y_recv,
+    cum_ref, y_ref, gates, direct, o1, m1, l1, o_send, o_recv, y_send, y_recv,
     in_sem, a_sem, q_sem, kv_sem, g_sem, z_ss, z_rs, p1_sem, p2_ss, p2_rs, p3_sem, o_sem, y_sem,
 ):
     seq, tp = lax.axis_index("seq"), lax.axis_index("tp")
@@ -101,7 +101,9 @@
             [a[:, (first + j) * 128:(first + j + 1) * 128] for j in range(count)], 0
         ).astype(BF16)
 
-    dec_block = jnp.concatenate([dec, dec], 0).astype(BF16)
+    place_at = (seq * TP + tp) * 8 + lax.broadcasted_iota(jnp.int32, (8, 128), 0)
+    dec = jnp.where(place_at >= start_ref[0], dec, 0.0)
+    dec_block = jnp.concatenate([dec, in_weights(dec)], 0).astype(BF16)
     for t in range(TP):
         at = slice(t * 128, (t + 1) * 128)
         bc_block = jnp.concatenate([bb[:, at], cc[:, at]], 0).astype(BF16)
@@ -231,8 +233,8 @@
     others = (-1, 1, -3, 3, -5, 5, -7, 7, 8)
 
     over_tp(lambda t: kv_copy(t, tp).start())
+    begin(cache, 0, False)
     over_plane(lambda d: a_copy(d, me).start())
-    begin(cache, 0, False)
     over_plane(lambda d: q_copy(d, me).start())
     over_tp(lambda t: g_copy(t, tp).start())
 
@@ -244,27 +246,27 @@
     fresh[z, 64:128, :] = kv[:, 8:16, :].reshape(64, DH).astype(BF16)
     begin(fresh, 1, True)
     forward(cache, 0, 2, False)
-    settle(a_recv, a_sem.at[1], PLANE - 1)
-    forward(fresh, 1, 1, True)
-
-    def halves(first_row):
-        part = a_recv[:, first_row:first_row + 16, :].astype(F32)
-        return part[:, 0:8, :].reshape(SPAN, 128), part[:, 8:16, :].reshape(SPAN, 128)
-
     row = lax.broadcasted_iota(jnp.int32, (SPAN, SPAN), 0)
     col = lax.broadcasted_iota(jnp.int32, (SPAN, SPAN), 1)
     lower = row >= col
     ones = lower.astype(F32).astype(BF16)
-    b_all, c_all = halves(16)
-    b_all, c_all = b_all.astype(BF16), c_all.astype(BF16)
     mine = (
         lax.broadcasted_iota(jnp.int32, (128, SPAN), 0)
         == tp * 16 + lane * 4 + lax.broadcasted_iota(jnp.int32, (128, SPAN), 1) // P_SIZE
     )
-    decay = dot(halves(32)[0].astype(BF16), mine.astype(F32).astype(BF16), 1, 0)
-    decay = jnp.where(z * SPAN + row >= start_ref[0], decay, 0.0)
-    d_all = decay.astype(BF16)
-    x_all = jnp.concatenate(halves(0), 1) * in_weights(decay)
+    mine = mine.astype(F32).astype(BF16)
+    forward(fresh, 1, 1, True)
+    settle(a_recv, a_sem.at[1], PLANE - 1)
+
+    def halves(first_row):
+        part = a_recv[:, first_row:first_row + 16, :].astype(F32)
+        return part[:, 0:8, :].reshape(SPAN, 128), part[:, 8:16, :].reshape(SPAN, 128)
+
+    b_all, c_all = halves(16)
+    b_all, c_all = b_all.astype(BF16), c_all.astype(BF16)
+    decays, weights = halves(32)
+    d_all = dot(decays.astype(BF16), mine, 1, 0).astype(BF16)
+    x_all = jnp.concatenate(halves(0), 1) * dot(weights.astype(BF16), mine, 1, 0)
     cum = dot(ones, d_all, 1, 0)
     end = cum[SPAN - 1:SPAN, :]
     local = dot((x_all * jnp.exp(end - cum)).astype(BF16), b_all, 0, 0).astype(BF16)
@@ -356,16 +358,15 @@
 
     loads[10].wait()
     pl.when(four == 0)(spread)
-    forward(fresh, 1, 3, True)
 
     key_at = lax.broadcasted_iota(jnp.int32, (1, KEYS), 1)
     key_place = (key_at // 64) * SPAN + lane * 64 + lax.rem(key_at, 64)
     row_at = lax.broadcasted_iota(jnp.int32, (UNIT, 1), 0)
 
-    def part(u, buf, usable):
+    def part(u, buf, usable, blocks=Z):
         queries = q_recv[pl.ds(u * 8, 8)].reshape(UNIT, DH)
-        keys = buf[:, 0:64, :].reshape(KEYS, DH)
-        values = buf[:, 64:128, :].reshape(KEYS, DH)
+        keys = buf[0:blocks, 0:64, :].reshape(blocks * 64, DH)
+        values = buf[0:blocks, 64:128, :].reshape(blocks * 64, DH)
         scores = jnp.where(usable, dot(queries, keys, 1, 1) * SCALE, LOW)
         top = jnp.max(scores, axis=1, keepdims=True)
         weights = jnp.exp(scores - top)
@@ -381,6 +382,8 @@
         m1[u * UNIT:(u + 1) * UNIT, :] = top
         l1[u * UNIT:(u + 1) * UNIT, :] = weight
         o1[u * UNIT:(u + 1) * UNIT, :] = mixed
+        if u == 1:
+            forward(fresh, 1, 3, True)
 
     pl.when(four > 0)(spread)
 
@@ -392,11 +395,12 @@
     ).astype(F32)
     spot_row = lax.broadcasted_iota(jnp.int32, (8, 16, 128), 1)
 
-    def unit(i, unused):
+    def unit(i, blocks):
         u = lax.rem(lane + 1 + i, LANES)
         query_place = z * SPAN + u * 64 + (row_at // 32) * 8 + lax.rem(row_at, 8)
-        usable = (key_place >= start_ref[0]) & (key_place <= query_place)
-        top, weight, mixed = part(u, fresh, usable)
+        places = key_place[:, 0:blocks * 64]
+        usable = (places >= start_ref[0]) & (places <= query_place)
+        top, weight, mixed = part(u, fresh, usable, blocks)
         rows = pl.ds(pl.multiple_of(u * UNIT, UNIT), UNIT)
         top1, weight1 = m1[rows, :], l1[rows, :]
         both = jnp.maximum(top, top1)
@@ -414,10 +418,13 @@
         for n in range(1, TP):
             o_copy(u * TP + lax.rem(tp + n, TP), me).start()
         pl.when(u != lane)(lambda: o_copy(u * TP + tp, me).start())
-        return unused
-
-    for i in range(LANES):
-        unit(i, 0)
+
+    def units(blocks):
+        for i in range(LANES):
+            unit(i, blocks)
+
+    pl.when(z < Z // 2)(lambda: units(Z // 2))
+    pl.when(z >= Z // 2)(lambda: units(Z))
     o_recv[me] = o_send[me]
 
     settle(p3_recv, p3_sem.at[1], 3)
@@ -429,6 +436,14 @@
     y_recv[me] = y_send[me]
     over_plane(lambda d: y_copy(d, me).start())
 
+    settle(g_recv, g_sem.at[1], TP - 1)
+    loads[11].wait()
+    for t in range(TP):
+        for r in range(8):
+            at = slice(t * 1024 + r * 128, t * 1024 + (r + 1) * 128)
+            gate = gate_ref[:, at].astype(F32)
+            gates[:, at] = gate / (1.0 + jnp.exp(-gate))
+            direct[:, at] = g_recv[t, 8 + r:9 + r, :] * x_ref[:, at].astype(F32)
     settle(o_recv, o_sem.at[1], PLANE - 1)
     for t in range(TP):
         sizes = []
@@ -446,8 +461,6 @@
             at = (t * 4 + h) * 128
             attn_ref[:, at:at + 128] = out[h * 8:(h + 1) * 8, :].astype(BF16)
 
-    settle(g_recv, g_sem.at[1], TP - 1)
-    loads[11].wait()
     settle(y_recv, y_sem.at[1], PLANE - 1)
     for t in range(TP):
         gated, squares = [], 0.0
@@ -456,11 +469,8 @@
             for half in range(2):
                 r = l * 2 + half
                 at = t * 1024 + r * 128
-                gate = gate_ref[:, at:at + 128].astype(F32)
-                value = y_part[half * 8:(half + 1) * 8, :] + g_recv[
-                    t, 8 + r:9 + r, :
-                ] * x_ref[:, at:at + 128].astype(F32)
-                value = value * (gate / (1.0 + jnp.exp(-gate)))
+                value = y_part[half * 8:(half + 1) * 8, :] + direct[:, at:at + 128]
+                value = value * gates[:, at:at + 128]
                 squares = squares + value * value
                 gated.append(value)
         scale = lax.rsqrt(jnp.sum(squares, axis=1, keepdims=True) * (1.0 / 1024) + 1e-5)
@@ -493,8 +503,8 @@
     return pl.pallas_call(
         kernel,
         out_shape=(
-            jax.ShapeDtypeStruct((8, 4096), BF16),
-            jax.ShapeDtypeStruct((8, 8192), BF16),
+            pltpu.VMEM((8, 4096), BF16),
+            pltpu.VMEM((8, 8192), BF16),
         ),
         in_specs=[smem] * 3 + [hbm] * 12,
         out_specs=(vmem, vmem),
@@ -528,6 +538,8 @@
             pltpu.VMEM((4, 64, 128), BF16),
             pltpu.VMEM((SPAN, SPAN), F32),
             pltpu.VMEM((SPAN, SPAN), F32),
+            pltpu.VMEM((8, 8192), F32),
+            pltpu.VMEM((8, 8192), F32),
             pltpu.VMEM((ROWS, DH), F32),
             pltpu.VMEM((ROWS, 1), F32),
             pltpu.VMEM((ROWS, 1), F32),

time: 54.8 us -> 51.7 us (0.943)
  Pallas kernels: 50.5 us -> 48.3 us
  local copies, waits for them, and re-layouts: 2.17 us -> 1.29 us
    pallas_call x1, Pallas kernels: 50.5 us -> 48.3 us  [local(): pl.pallas_call(kernel, out_shape=(pltpu.VMEM((8, 4096), BF16), pltpu.VMEM...]
    unnamed x4 -> x2, local copies, waits for them, and re-layouts: 2.17 us -> 1.29 us
where the time goes in v4:
time: 51.7 us; the launch traced here: 51.5 us
  Pallas kernels  48.3 us (93%)
  between operations  1.94 us (4%)
  local copies, waits for them, and re-layouts  1.29 us (2%)
    pallas_call x1, Pallas kernels, local(): pl.pallas_call(kernel, out_shape=(pltpu.VMEM((8, 4096), BF16), pltpu.VMEM...  48.3 us
    unnamed x2, local copies, waits for them, and re-layouts  1.29 us

profile of v4, /device:TPU:1, one launch (start us, length us, event | category | flops | bytes accessed | tf_op | source)
XLA Modules:
  0.0 51.5 jit_solution(2323469236696152905)
XLA Ops:
  1.9 48.3 %mixers.1 = (bf16[8,4096]{1,0:T(8,128)(2,1)S(1)}, bf16[8,8192]{1,0:T(8,128)(2,1)S(1)}) custom-call(s32[1]{0:T(128)S(6)} %copy.21.length_ref, s32[1]{0:T(128)S(6)} %copy.22.start_ref, f32[16]{0:T(128)} %skip_ref.1, bf16[8,4096]{1,0:T(8,128)(2,1)} %q_hbm.1, bf16[8,1024]{1,0:T(8,128)(2,1)} %k_hbm.1, bf16[8,1024]{1,0:T(8,128)(2,1)} %v_hbm.1, ...), custom_call_target="tpu_custom_call" | custom-call | tf_op jit(solution)/shard_map/mixers/pallas_call | solution.py:503
  50.2 0.6 %copy.19 = bf16[8,4096]{1,0:T(8,128)(2,1)} copy(bf16[8,4096]{1,0:T(8,128)(2,1)S(1)} %get-tuple-element.2) | data formatting | bytes 131072
  50.9 0.7 %copy.20 = bf16[8,8192]{1,0:T(8,128)(2,1)} copy(bf16[8,8192]{1,0:T(8,128)(2,1)S(1)} %get-tuple-element.3) | data formatting | bytes 262144

commit v5 on v4

--- a/solution.py
+++ b/solution.py
@@ -44,7 +44,7 @@
     a_send, a_recv, q_send, q_recv, kv_send, kv_recv, g_recv, cache, fresh,
     p1_send, p1_recv, p2_send, p2_recv, p3_send, p3_recv,
     cum_ref, y_ref, gates, direct, o1, m1, l1, o_send, o_recv, y_send, y_recv,
-    in_sem, a_sem, q_sem, kv_sem, g_sem, z_ss, z_rs, p1_sem, p2_ss, p2_rs, p3_sem, o_sem, y_sem,
+    in_sem, a_sem, q_sem, kv_sem, g_sem, z_ss, z_rs, p1_sem, p2_ss, p2_rs, p3_sem, o_sem, y_sem, ready,
 ):
     seq, tp = lax.axis_index("seq"), lax.axis_index("tp")
     z, lane = seq // LANES, lax.rem(seq, LANES)
@@ -80,10 +80,16 @@
         )
         return unused
 
-    offsets = [k for k in range(-REACH, REACH + 1) if k] + [8]
+    offsets = [k for k in range(-REACH, REACH + 1) if k]
     for k in offsets:
         pl.semaphore_signal(barrier, inc=1, device_id=along(k), device_id_type=MESH)
     lax.fori_loop(1, PLANE, greet, 0)
+    early = z < Z // 2
+
+    @pl.when(early)
+    def greet_far():
+        pl.semaphore_signal(barrier, inc=1, device_id=along(8), device_id_type=MESH)
+
 
     for load in loads[:8]:
         load.wait()
@@ -128,7 +134,12 @@
         skips = jnp.where(tile_row * 2 + tile_lane // P_SIZE == h, skip_ref[h], skips)
     gain_ref[8:16, :] = skips
     g_recv[tp] = gain_ref[...]
-    pl.semaphore_wait(barrier, PLANE - 1 + len(offsets))
+    pl.semaphore_wait(barrier, PLANE - 1 + len(offsets) + jnp.where(early, 0, 1))
+
+    @pl.when(z >= Z // 2)
+    def answer():
+        pl.semaphore_signal(ready, inc=1, device_id=along(8), device_id_type=MESH)
+
 
     def copy(src, dst, send, recv, device):
         return pltpu.make_async_remote_copy(
@@ -335,6 +346,7 @@
         total, total_log = total * jnp.exp(log) + add, total_log + log
     p2_send[0:64, :] = total.astype(BF16)
     p2_send[64:80, :] = log_rows(total_log)
+    pl.when(early)(lambda: pl.semaphore_wait(ready, 1))
     for k in (1, 2, 3):
         pl.when(four + k < 4)(lambda k=k: p2_copy(four + k, four).start())
 
@@ -550,6 +562,7 @@
             dma((12,)), dma((2,)), dma((2,)), dma((2,)), dma((2,)),
             dma((2, 16)), dma((2, Z)),
             dma((2,)), dma((4,)), dma((4,)), dma((2,)), dma((2,)), dma((2,)),
+            pltpu.SemaphoreType.REGULAR,
         ],
         compiler_params=pltpu.CompilerParams(
             collective_id=0, has_side_effects=True, vmem_limit_bytes=56 * 1024 * 1024

time: 51.7 us -> 50.4 us (0.975)
  Pallas kernels: 48.3 us -> 47.1 us
    pallas_call x1, Pallas kernels: 48.3 us -> 47.1 us  [local(): pl.pallas_call(kernel, out_shape=(pltpu.VMEM((8, 4096), BF16), pltpu.VMEM...]
where the time goes in v5:
time: 50.4 us; the launch traced here: 50.3 us
  Pallas kernels  47.1 us (93%)
  between operations  1.94 us (4%)
  local copies, waits for them, and re-layouts  1.29 us (3%)
    pallas_call x1, Pallas kernels, local(): pl.pallas_call(kernel, out_shape=(pltpu.VMEM((8, 4096), BF16), pltpu.VMEM...  47.1 us
    unnamed x2, local copies, waits for them, and re-layouts  1.29 us

profile of v5, /device:TPU:1, one launch (start us, length us, event | category | flops | bytes accessed | tf_op | source)
XLA Modules:
  0.0 50.3 jit_solution(2947060370818596770)
XLA Ops:
  1.9 47.1 %mixers.1 = (bf16[8,4096]{1,0:T(8,128)(2,1)S(1)}, bf16[8,8192]{1,0:T(8,128)(2,1)S(1)}) custom-call(s32[1]{0:T(128)S(6)} %copy.21.length_ref, s32[1]{0:T(128)S(6)} %copy.22.start_ref, f32[16]{0:T(128)} %skip_ref.1, bf16[8,4096]{1,0:T(8,128)(2,1)} %q_hbm.1, bf16[8,1024]{1,0:T(8,128)(2,1)} %k_hbm.1, bf16[8,1024]{1,0:T(8,128)(2,1)} %v_hbm.1, ...), custom_call_target="tpu_custom_call" | custom-call | tf_op jit(solution)/shard_map/mixers/pallas_call | solution.py:515
  49.0 0.6 %copy.19 = bf16[8,4096]{1,0:T(8,128)(2,1)} copy(bf16[8,4096]{1,0:T(8,128)(2,1)S(1)} %get-tuple-element.2) | data formatting | bytes 131072
  49.6 0.7 %copy.20 = bf16[8,8192]{1,0:T(8,128)(2,1)} copy(bf16[8,8192]{1,0:T(8,128)(2,1)S(1)} %get-tuple-element.3) | data formatting | bytes 262144
